TPU v7x, 512 devices: a whole 4x8x8 slice. The times are simulated.
512 devices in a mesh: dom: 128 (over z, y, core), feat: 4 (over x).
Axes of the slice: x: 4, y: 8, z: 8, core: 2. Of those that a mesh axis runs over, the one named last changes fastest.
Arguments:
- grad_pre2: bfloat16 [262144, 512], P('dom', 'feat'), may hold values from -6 to 6
- aggregated2: bfloat16 [262144, 512], P('dom', 'feat'), may hold values from -6 to 6
- weight2: bfloat16 [512, 512], P('feat'), may hold values from -0.25 to 0.25
- pre1: bfloat16 [262144, 512], P('dom', 'feat'), may hold values from -6 to 6
- aggregated1: bfloat16 [262144, 512], P('dom', 'feat'), may hold values from -6 to 6
- weight1: bfloat16 [512, 512], P('feat'), may hold values from -0.25 to 0.25
- blocks: bfloat16 [2048, 6, 128, 128], P('dom'), may hold values from -0.21875 to 0.21875
- targets: int32 [2048, 6], P('dom'), may hold values from 0 to 2047, as said below
Outputs:
- grad_weight2: float32 [512, 512], P('feat')
- grad_weight1: float32 [512, 512], P('feat')
- grad_input: bfloat16 [262144, 512], P('dom', 'feat')
Inputs may be any that keep to these rules, and one draw needn't show every extreme that they name: `targets`: partition p holds row tiles p * 16 to p * 16 + 15. Entry 0 of a row tile's list is the tile itself. Every other entry names a tile of partition p + o with -2 <= o <= 2: one of that partition's last 8 tiles if o < 0, one of its first 8 tiles if o > 0, any of its tiles if o = 0. The first row tile of every partition names partitions p - 2, p - 1, p + 1 and p + 2 wherever they exist; the number of blocks that name another partition varies from tile to tile.
All inputs are finite; a program needn't handle non-finite values.
Results may differ from a plain program's by a relative error of at most 0.015.
Values may be sent and summed in bfloat16 or wider, within the bound.
A program may use at most 64 MiB of HBM per device.

v0:
```python
import math

import jax
import jax.numpy as jnp
from jax import lax
from jax.sharding import Mesh
from jax.sharding import PartitionSpec as P

REACH = 2
DOM = ("dom_0", "dom_1", "dom_2")


def in_order(tiles, dim):
    shape = list(tiles.shape[1:])
    shape[dim] *= tiles.shape[0]
    return jnp.moveaxis(tiles, 0, dim).reshape(shape)


def from_everyone(array, axis):
    copies = jnp.broadcast_to(array, (lax.axis_size(axis), *array.shape))
    return lax.all_to_all(copies, axis, split_axis=0, concat_axis=0, tiled=True)


def gather_directly(array, axis, dim):
    return in_order(from_everyone(array, axis), dim)


def from_behind(value, axis, steps):
    count = lax.axis_size(axis)
    initial, last = (max(0, -steps), min(count, count - steps))
    return lax.ppermute(value, axis, [(source, source + steps) for source in range(initial, last)])


def cut_along(array, dim, size):
    before, after = (array.shape[:dim], array.shape[dim + 1 :])
    return jnp.moveaxis(array.reshape(*before, size, -1, *after), dim, 0)


def summed_on_arrival(array, axis, dim):
    tiles = cut_along(array, dim, lax.axis_size(axis))
    arrived = lax.all_to_all(tiles, axis, split_axis=0, concat_axis=0, tiled=True)
    return arrived.sum(axis=0)


def sum_in_two_steps(array, axes, dim):
    far, near = axes
    own = summed_on_arrival(cut_along(array, dim, lax.axis_size(far)), near, dim + 1)
    return jnp.sum(lax.all_to_all(own, far, 0, 0, tiled=True), axis=0)


def rows_for(lines, size):
    spare = -lines.shape[0] % size
    if not spare:
        return lines
    return jnp.concatenate([lines, jnp.zeros((spare, *lines.shape[1:]), lines.dtype)])


def whole_of(array, axes, dim):
    far, near = axes
    initial = from_everyone(array, far)
    tiles = jnp.swapaxes(from_everyone(initial, near), 0, 1)
    return in_order(tiles.reshape(-1, *array.shape), dim)


def total_of(array, axes):
    own = sum_in_two_steps(
        rows_for(array, lax.axis_size(axes[0]) * lax.axis_size(axes[1])), axes, 0
    )
    whole = whole_of(own, axes, 0)
    return whole[: len(array)].reshape(array.shape)


def packed_total(arrays, axis):
    line, at, finished = (jnp.concatenate([a.reshape(-1) for a in arrays]), 0, [])
    subtotal = total_of(line, axis)
    for a in arrays:
        finished.append(subtotal[at : at + a.size].reshape(a.shape))
        at += a.size
    return tuple(finished)


def dense_backward(grad_pre, aggregated, weight, grad_scale):
    columns = gather_directly(grad_pre, "feat", 1)
    running = lax.dot_general(
        columns, weight, (((1,), (1,)), ((), ())), preferred_element_type=jnp.float32
    )
    term_part = (
        lax.dot_general(
            aggregated, columns, (((0,), (0,)), ((), ())), preferred_element_type=jnp.float32
        )
        * grad_scale
    )
    weight_grad = term_part
    running, weight_grad = (running, weight_grad)
    return (running.astype(jnp.bfloat16), weight_grad)


def spread_tiles(values, blocks, targets):
    tile_count = blocks.shape[0]
    count = blocks.shape[1]
    tile_size = blocks.shape[2]
    col_count = values.shape[1]
    sources = values.reshape(tile_count, tile_size, col_count)
    products = jnp.einsum("rkij,rjc->rkic", blocks, sources, preferred_element_type=jnp.float32)
    first_tile = lax.axis_index(DOM) * tile_count
    relative = targets.reshape(-1) - first_tile + REACH * tile_count
    summed = jax.ops.segment_sum(
        products.reshape(tile_count * count, tile_size, col_count),
        relative,
        num_segments=(2 * REACH + 1) * tile_count,
    )
    half = tile_count // 2
    owned = summed[REACH * tile_count : (REACH + 1) * tile_count]
    lower_half = owned[:half]
    upper_half = owned[half:]
    upward_parts = [
        summed[(REACH + distance) * tile_count : (REACH + distance) * tile_count + half].astype(
            jnp.bfloat16
        )
        for distance in range(1, REACH + 1)
    ]
    downward_parts = [
        summed[
            (REACH - distance + 1) * tile_count - half : (REACH - distance + 1) * tile_count
        ].astype(jnp.bfloat16)
        for distance in range(1, REACH + 1)
    ]
    for distance in range(1, REACH + 1):
        lower_half = lower_half + from_behind(upward_parts[distance - 1], DOM, distance).astype(
            jnp.float32
        )
        upper_half = upper_half + from_behind(downward_parts[distance - 1], DOM, -distance).astype(
            jnp.float32
        )
    return jnp.concatenate([lower_half, upper_half], axis=0).reshape(
        tile_count * tile_size, col_count
    )


def shards(grad_pre2, aggregated2, weight2, pre1, aggregated1, weight1, blocks, targets):
    grad_scale = 1.0 / math.sqrt(grad_pre2.shape[0] * lax.axis_size(DOM))
    grad_agg2, second_part = dense_backward(grad_pre2, aggregated2, weight2, grad_scale)
    grad_hidden1 = spread_tiles(grad_agg2, blocks, targets)
    grad_pre1 = jnp.where(pre1 > 0, grad_hidden1, 0.0).astype(jnp.bfloat16)
    grad_agg1, first_part = dense_backward(grad_pre1, aggregated1, weight1, grad_scale)
    grad_input = spread_tiles(grad_agg1, blocks, targets).astype(jnp.bfloat16)
    grad_weight2, grad_weight1 = packed_total(
        (second_part, first_part), (("dom_0", "dom_1"), "dom_2")
    )
    return (grad_weight2, grad_weight1, grad_input)


def solution(mesh):
    split = Mesh(
        mesh.devices.reshape(8, 8, 2, mesh.shape["feat"]), ("dom_0", "dom_1", "dom_2", "feat")
    )
    placed = (
        P(DOM, "feat"),
        P(DOM, "feat"),
        P("feat", None),
        P(DOM, "feat"),
        P(DOM, "feat"),
        P("feat", None),
        P(DOM, None, None, None),
        P(DOM, None),
    )
    return jax.shard_map(
        shards,
        mesh=split,
        in_specs=placed,
        out_specs=(P("feat", None), P("feat", None), P(DOM, "feat")),
        check_vma=False,
    )
```

profile of v0, /device:TPU:1, one launch (start us, length us, event | category | flops | bytes accessed | tf_op | source)
XLA Modules:
  0.0 251.7 jit_solution(1392617836701030422)
XLA Ops:
  0.6 2.2 copy.31
  2.8 2.7 %broadcast_in_dim.18 = bf16[4,2048,128]{1,2,0:T(8,128)(2,1)} broadcast(bf16[2048,128]{0,1:T(8,128)(2,1)} %copy.31), dimensions={1,2} | broadcast | bytes 2621440 | tf_op jit(solution)/shard_map/broadcast_in_dim | solution.py:20
  5.5 4.8 %all-to-all-start = ((bf16[4,2048,128]{1,2,0:T(8,128)(2,1)}), bf16[4,2048,128]{1,2,0:T(8,128)(2,1)}, u32[]{:S(2)}, u32[]{:S(2)}) async-start(bf16[4,2048,128]{1,2,0:T(8,128)(2,1)} %broadcast_in_dim.18), calls=%async_computation | async-start | bytes 4194304 | tf_op jit(solution)/shard_map/all_to_all | solution.py:21
  10.5 19.9 %all-to-all-done = bf16[4,2048,128]{1,2,0:T(8,128)(2,1)} async-done(((bf16[4,2048,128]{1,2,0:T(8,128)(2,1)}), bf16[4,2048,128]{1,2,0:T(8,128)(2,1)}, u32[]{:S(2)}, u32[]{:S(2)}) %all-to-all-start) | async-done | bytes 2097184 | tf_op jit(solution)/shard_map/all_to_all | solution.py:21
  30.5 2.3 convolution_convert_fusion.1
  32.8 3.7 %fusion.11 = f32[16,128,6,128]{3,1,2,0:T(8,128)} fusion(bf16[16,128,128,1]{2,1,3,0:T(8,128)(2,1)S(1)} %bitcast.50, bf16[16,6,128,128]{3,2,1,0:T(8,128)(2,1)S(1)} %copy-done), kind=kOutput, calls=%fused_computation.27 | convolution fusion | flops 402653184 | bytes 9961472 | tf_op jit(solution)/shard_map/rkij,rjc->rkic/dot_general | solution.py:104
  36.5 6.6 %copy.34 = f32[96,128,128]{2,1,0:T(8,128)} copy(f32[96,128,128]{1,2,0:T(8,128)} %bitcast.47) | data formatting | bytes 12582912 | tf_op jit(solution)/shard_map/reshape | solution.py:108
  43.1 3.0 %broadcast.35.clone = f32[80,128,128]{2,1,0:T(8,128)} broadcast(f32[]{:T(128)} %constant.8.clone.1), dimensions={} | broadcast | bytes 5242884 | tf_op jit(solution)/shard_map/broadcast.3
  46.1 20.2 %scatter_fusion = f32[80,128,128]{2,1,0:T(8,128)} fusion(f32[80,128,128]{2,1,0:T(8,128)} %broadcast.35.clone, s32[96]{0:T(128)S(1)} %reshape.81, f32[96,128,128]{2,1,0:T(8,128)} %copy.34), kind=kCustom, calls=%fused_computation | custom fusion | flops 1572864 | bytes 18874752 | tf_op jit(solution)/shard_map/scatter-add | solution.py:107
  66.3 3.0 %convert.18 = bf16[80,128,128]{2,1,0:T(8,128)(2,1)S(1)} convert(f32[80,128,128]{2,1,0:T(8,128)} %scatter_fusion) | non-fusion elementwise | flops 1310720 | bytes 7864320 | tf_op jit(solution)/shard_map/convert.9
  69.4 9.3 %collective-permute-start.1 = (bf16[8,128,128]{2,1,0:T(8,128)(2,1)S(1)}, bf16[8,128,128]{2,1,0:T(8,128)(2,1)S(1)}, u32[]{:S(2)}, u32[]{:S(2)}) collective-permute-start(bf16[8,128,128]{2,1,0:T(8,128)(2,1)S(1)} %get-tuple-element.14), channel_id=1, source_target_pairs={{0,8},{4,12},{8,16},{12,20},{16,24},{20,28},{24,32},{28,36},{32,40... | collective-permute-start | bytes 786440 | tf_op jit(solution)/shard_map/ppermute | solution.py:31
  78.8 5.2 %collective-permute-start = (bf16[8,128,128]{2,1,0:T(8,128)(2,1)S(1)}, bf16[8,128,128]{2,1,0:T(8,128)(2,1)S(1)}, u32[]{:S(2)}, u32[]{:S(2)}) collective-permute-start(bf16[8,128,128]{2,1,0:T(8,128)(2,1)S(1)} %get-tuple-element.11), channel_id=1, source_target_pairs={{0,4},{4,8},{8,12},{12,16},{16,20},{20,24},{24,28},{28,32},{32,36}... | collective-permute-start | bytes 786440 | tf_op jit(solution)/shard_map/ppermute | solution.py:31
  87.7 6.2 %collective-permute-done.3 = bf16[8,128,128]{2,1,0:T(8,128)(2,1)S(1)} collective-permute-done((bf16[8,128,128]{2,1,0:T(8,128)(2,1)S(1)}, bf16[8,128,128]{2,1,0:T(8,128)(2,1)S(1)}, u32[]{:S(2)}, u32[]{:S(2)}) %collective-permute-start.3) | collective-permute-done | bytes 262176 | tf_op jit(solution)/shard_map/ppermute | solution.py:31
  98.0 2.0 copy.35
  100.1 2.6 %broadcast_in_dim.20 = bf16[4,2048,128]{1,2,0:T(8,128)(2,1)} broadcast(bf16[2048,128]{0,1:T(8,128)(2,1)} %copy.35), dimensions={1,2} | broadcast | bytes 2621440 | tf_op jit(solution)/shard_map/broadcast_in_dim | solution.py:20
  102.7 4.4 %all-to-all-start.1 = ((bf16[4,2048,128]{1,2,0:T(8,128)(2,1)}), bf16[4,2048,128]{1,2,0:T(8,128)(2,1)}, u32[]{:S(2)}, u32[]{:S(2)}) async-start(bf16[4,2048,128]{1,2,0:T(8,128)(2,1)} %broadcast_in_dim.20), calls=%async_computation.1 | async-start | bytes 4194304 | tf_op jit(solution)/shard_map/all_to_all | solution.py:21
  107.1 2.6 %convolution_multiply_fusion.1 = f32[128,512]{1,0:T(8,128)S(1)} fusion(bf16[2048,128]{1,0:T(8,128)(2,1)} %param.9, bf16[2048,512]{0,1:T(8,128)(2,1)} %bitcast.1), kind=kOutput, calls=%fused_computation.6 | convolution fusion | flops 268500992 | bytes 2883584 | tf_op jit(solution)/shard_map/dot_general | solution.py:88
  110.6 20.3 %all-to-all-done.1 = bf16[4,2048,128]{1,2,0:T(8,128)(2,1)} async-done(((bf16[4,2048,128]{1,2,0:T(8,128)(2,1)}), bf16[4,2048,128]{1,2,0:T(8,128)(2,1)}, u32[]{:S(2)}, u32[]{:S(2)}) %all-to-all-start.1) | async-done | bytes 2097184 | tf_op jit(solution)/shard_map/all_to_all | solution.py:21
  131.0 3.1 %fusion = f32[128,512]{0,1:T(8,128)} fusion(bf16[2048,512]{0,1:T(8,128)(2,1)} %bitcast.9, bf16[2048,128]{1,0:T(8,128)(2,1)} %param.12), kind=kOutput, calls=%fused_computation.5 | convolution fusion | flops 268500992 | bytes 2883584 | tf_op jit(solution)/shard_map/dot_general | solution.py:88
  137.5 4.5 %all_to_all.38 = f32[2,64,1024]{2,1,0:T(8,128)} all-to-all(f32[2,64,1024]{2,1,0:T(8,128)S(1)} %copy.37), channel_id=1, replica_groups=mesh['dom_0'=8,'dom_1'=8,'dom_2'=2,'feat'=4] {'dom_2'}, dimensions={0} | all-to-all | bytes 1048576 | tf_op jit(solution)/shard_map/all_to_all | solution.py:41
  144.0 19.3 %all-to-all-start.3 = ((f32[64,1,1024]{2,1,0:T(1,128)}), f32[64,1,1024]{2,1,0:T(1,128)S(1)}, u32[]{:S(2)}, u32[]{:S(2)}) async-start(f32[64,1,1024]{2,1,0:T(1,128)} %all_to_all.27), calls=%async_computation.3 | async-start | bytes 524288 | tf_op jit(solution)/shard_map/all_to_all | solution.py:48
  163.4 2.4 convolution_convert_fusion
  165.7 3.7 %fusion.12 = f32[16,128,6,128]{3,1,2,0:T(8,128)} fusion(bf16[16,128,128,1]{2,1,3,0:T(8,128)(2,1)S(1)} %bitcast.49, bf16[16,6,128,128]{3,2,1,0:T(8,128)(2,1)S(1)} %copy-done), kind=kOutput, calls=%fused_computation.28 | convolution fusion | flops 402653184 | bytes 9961472 | tf_op jit(solution)/shard_map/rkij,rjc->rkic/dot_general | solution.py:104
  169.4 6.6 %copy.41 = f32[96,128,128]{2,1,0:T(8,128)} copy(f32[96,128,128]{1,2,0:T(8,128)} %bitcast.48) | data formatting | bytes 12582912 | tf_op jit(solution)/shard_map/reshape | solution.py:108
  176.0 3.0 %broadcast.35 = f32[80,128,128]{2,1,0:T(8,128)} broadcast(f32[]{:T(128)} %constant.8.clone.1), dimensions={} | broadcast | bytes 5242884 | tf_op jit(solution)/shard_map/broadcast.3
  179.0 20.2 %scatter_fusion.1 = f32[80,128,128]{2,1,0:T(8,128)} fusion(f32[80,128,128]{2,1,0:T(8,128)} %broadcast.35, s32[96]{0:T(128)S(1)} %reshape.81, f32[96,128,128]{2,1,0:T(8,128)} %copy.41), kind=kCustom, calls=%fused_computation.1 | custom fusion | flops 1572864 | bytes 18874752 | tf_op jit(solution)/shard_map/scatter-add | solution.py:107
  199.2 3.0 %convert.19 = bf16[80,128,128]{2,1,0:T(8,128)(2,1)S(1)} convert(f32[80,128,128]{2,1,0:T(8,128)} %scatter_fusion.1) | non-fusion elementwise | flops 1310720 | bytes 7864320 | tf_op jit(solution)/shard_map/convert.5
  203.2 3.3 %collective-permute-start.5 = (bf16[8,128,128]{2,1,0:T(8,128)(2,1)}, bf16[8,128,128]{2,1,0:T(8,128)(2,1)}, u32[]{:S(2)}, u32[]{:S(2)}) collective-permute-start(bf16[8,128,128]{2,1,0:T(8,128)(2,1)} %get-tuple-element.10), channel_id=1, source_target_pairs={{0,8},{4,12},{8,16},{12,20},{16,24},{20,28},{24,32},{28,36},{32,40... | collective-permute-start | bytes 786440 | tf_op jit(solution)/shard_map/ppermute | solution.py:31
  206.5 3.7 %collective-permute-start.4 = (bf16[8,128,128]{2,1,0:T(8,128)(2,1)}, bf16[8,128,128]{2,1,0:T(8,128)(2,1)}, u32[]{:S(2)}, u32[]{:S(2)}) collective-permute-start(bf16[8,128,128]{2,1,0:T(8,128)(2,1)} %get-tuple-element.7), channel_id=1, source_target_pairs={{0,4},{4,8},{8,12},{12,16},{16,20},{20,24},{24,28},{28,32},{32,36}... | collective-permute-start | bytes 786440 | tf_op jit(solution)/shard_map/ppermute | solution.py:31
  214.5 13.5 %all-to-all-start.4 = ((f32[64,1,1024]{2,1,0:T(1,128)}), f32[64,1,1024]{2,1,0:T(1,128)S(1)}, u32[]{:S(2)}, u32[]{:S(2)}) async-start(f32[64,1,1024]{2,1,0:T(1,128)} %broadcast_in_dim.21), calls=%async_computation.4 | async-start | bytes 524288 | tf_op jit(solution)/shard_map/all_to_all | solution.py:21
  230.5 9.9 %all-to-all-done.4 = f32[64,1,1024]{2,1,0:T(1,128)S(1)} async-done(((f32[64,1,1024]{2,1,0:T(1,128)}), f32[64,1,1024]{2,1,0:T(1,128)S(1)}, u32[]{:S(2)}, u32[]{:S(2)}) %all-to-all-start.4) | async-done | bytes 262176 | tf_op jit(solution)/shard_map/all_to_all | solution.py:21
  240.6 7.2 %all_to_all.39 = f32[2,64,1024]{2,1,0:T(8,128)S(1)} all-to-all(f32[2,64,1024]{2,1,0:T(8,128)S(1)} %broadcast_in_dim.22), channel_id=1, replica_groups=mesh['dom_0'=8,'dom_1'=8,'dom_2'=2,'feat'=4] {'dom_2'}, dimensions={0} | all-to-all | bytes 1048576 | tf_op jit(solution)/shard_map/all_to_all | solution.py:21
  (48 shorter events, 26.2 us)
Async XLA Ops:
  0.6 32.2 %copy-start = (bf16[16,6,128,128]{3,2,1,0:T(8,128)(2,1)S(1)}, bf16[16,6,128,128]{3,2,1,0:T(8,128)(2,1)}, u32[]{:S(2)}) copy-start(bf16[16,6,128,128]{3,2,1,0:T(8,128)(2,1)} %param.14) | copy-start | bytes 9437188
  2.8 7.5 %copy-start.4 = (s32[16,6]{0,1:T(8,128)S(1)}, s32[16,6]{0,1:T(8,128)}, u32[]{:S(2)}) copy-start(s32[16,6]{0,1:T(8,128)} %param.15) | copy-start | bytes 1156
  2.8 27.6 %copy-start.2 = (bf16[128,512]{1,0:T(8,128)(2,1)S(1)}, bf16[128,512]{1,0:T(8,128)(2,1)}, u32[]{:S(2)}) copy-start(bf16[128,512]{1,0:T(8,128)(2,1)} %param.10) | copy-start | bytes 393220
  5.5 24.9 %all-to-all-start = ((bf16[4,2048,128]{1,2,0:T(8,128)(2,1)}), bf16[4,2048,128]{1,2,0:T(8,128)(2,1)}, u32[]{:S(2)}, u32[]{:S(2)}) async-start(bf16[4,2048,128]{1,2,0:T(8,128)(2,1)} %broadcast_in_dim.18), calls=%async_computation | async-start | bytes 4194304 | tf_op jit(solution)/shard_map/all_to_all | solution.py:21
  69.3 27.7 %copy-start.1 = (bf16[2048,128]{1,0:T(8,128)(2,1)S(1)}, bf16[2048,128]{1,0:T(8,128)(2,1)}, u32[]{:S(2)}) copy-start(bf16[2048,128]{1,0:T(8,128)(2,1)} %param.11) | copy-start | bytes 1572868
  69.4 17.7 %collective-permute-start.1 = (bf16[8,128,128]{2,1,0:T(8,128)(2,1)S(1)}, bf16[8,128,128]{2,1,0:T(8,128)(2,1)S(1)}, u32[]{:S(2)}, u32[]{:S(2)}) collective-permute-start(bf16[8,128,128]{2,1,0:T(8,128)(2,1)S(1)} %get-tuple-element.14), channel_id=1, source_target_pairs={{0,8},{4,12},{8,16},{12,20},{16,24},{20,28},{24,32},{28,36},{32,40... | collective-permute-start | bytes 786440 | tf_op jit(solution)/shard_map/ppermute | solution.py:31
  78.8 8.9 %collective-permute-start = (bf16[8,128,128]{2,1,0:T(8,128)(2,1)S(1)}, bf16[8,128,128]{2,1,0:T(8,128)(2,1)S(1)}, u32[]{:S(2)}, u32[]{:S(2)}) collective-permute-start(bf16[8,128,128]{2,1,0:T(8,128)(2,1)S(1)} %get-tuple-element.11), channel_id=1, source_target_pairs={{0,4},{4,8},{8,12},{12,16},{16,20},{20,24},{24,28},{28,32},{32,36}... | collective-permute-start | bytes 786440 | tf_op jit(solution)/shard_map/ppermute | solution.py:31
  84.0 9.9 %collective-permute-start.3 = (bf16[8,128,128]{2,1,0:T(8,128)(2,1)S(1)}, bf16[8,128,128]{2,1,0:T(8,128)(2,1)S(1)}, u32[]{:S(2)}, u32[]{:S(2)}) collective-permute-start(bf16[8,128,128]{2,1,0:T(8,128)(2,1)S(1)} %get-tuple-element.12), channel_id=1, source_target_pairs={{8,0},{12,4},{16,8},{20,12},{24,16},{28,20},{32,24},{36,28},{40,32... | collective-permute-start | bytes 786440 | tf_op jit(solution)/shard_map/ppermute | solution.py:31
  85.3 10.3 %collective-permute-start.2 = (bf16[8,128,128]{2,1,0:T(8,128)(2,1)S(1)}, bf16[8,128,128]{2,1,0:T(8,128)(2,1)S(1)}, u32[]{:S(2)}, u32[]{:S(2)}) collective-permute-start(bf16[8,128,128]{2,1,0:T(8,128)(2,1)S(1)} %get-tuple-element.13), channel_id=1, source_target_pairs={{4,0},{8,4},{12,8},{16,12},{20,16},{24,20},{28,24},{32,28},{36,32}... | collective-permute-start | bytes 786440 | tf_op jit(solution)/shard_map/ppermute | solution.py:31
  102.7 28.3 %all-to-all-start.1 = ((bf16[4,2048,128]{1,2,0:T(8,128)(2,1)}), bf16[4,2048,128]{1,2,0:T(8,128)(2,1)}, u32[]{:S(2)}, u32[]{:S(2)}) async-start(bf16[4,2048,128]{1,2,0:T(8,128)(2,1)} %broadcast_in_dim.20), calls=%async_computation.1 | async-start | bytes 4194304 | tf_op jit(solution)/shard_map/all_to_all | solution.py:21
  134.0 29.3 %copy-start.3 = (bf16[128,512]{1,0:T(8,128)(2,1)S(1)}, bf16[128,512]{1,0:T(8,128)(2,1)}, u32[]{:S(2)}) copy-start(bf16[128,512]{1,0:T(8,128)(2,1)} %param.13) | copy-start | bytes 393220
  144.0 69.4 %all-to-all-start.3 = ((f32[64,1,1024]{2,1,0:T(1,128)}), f32[64,1,1024]{2,1,0:T(1,128)S(1)}, u32[]{:S(2)}, u32[]{:S(2)}) async-start(f32[64,1,1024]{2,1,0:T(1,128)} %all_to_all.27), calls=%async_computation.3 | async-start | bytes 524288 | tf_op jit(solution)/shard_map/all_to_all | solution.py:48
  203.2 24.8 %collective-permute-start.5 = (bf16[8,128,128]{2,1,0:T(8,128)(2,1)}, bf16[8,128,128]{2,1,0:T(8,128)(2,1)}, u32[]{:S(2)}, u32[]{:S(2)}) collective-permute-start(bf16[8,128,128]{2,1,0:T(8,128)(2,1)} %get-tuple-element.10), channel_id=1, source_target_pairs={{0,8},{4,12},{8,16},{12,20},{16,24},{20,28},{24,32},{28,36},{32,40... | collective-permute-start | bytes 786440 | tf_op jit(solution)/shard_map/ppermute | solution.py:31
  206.5 21.5 %collective-permute-start.4 = (bf16[8,128,128]{2,1,0:T(8,128)(2,1)}, bf16[8,128,128]{2,1,0:T(8,128)(2,1)}, u32[]{:S(2)}, u32[]{:S(2)}) collective-permute-start(bf16[8,128,128]{2,1,0:T(8,128)(2,1)} %get-tuple-element.7), channel_id=1, source_target_pairs={{0,4},{4,8},{8,12},{12,16},{16,20},{20,24},{24,28},{28,32},{32,36}... | collective-permute-start | bytes 786440 | tf_op jit(solution)/shard_map/ppermute | solution.py:31
  210.2 17.8 %collective-permute-start.7 = (bf16[8,128,128]{2,1,0:T(8,128)(2,1)}, bf16[8,128,128]{2,1,0:T(8,128)(2,1)}, u32[]{:S(2)}, u32[]{:S(2)}) collective-permute-start(bf16[8,128,128]{2,1,0:T(8,128)(2,1)} %get-tuple-element.8), channel_id=1, source_target_pairs={{8,0},{12,4},{16,8},{20,12},{24,16},{28,20},{32,24},{36,28},{40,32... | collective-permute-start | bytes 786440 | tf_op jit(solution)/shard_map/ppermute | solution.py:31
  211.5 16.5 %collective-permute-start.6 = (bf16[8,128,128]{2,1,0:T(8,128)(2,1)}, bf16[8,128,128]{2,1,0:T(8,128)(2,1)}, u32[]{:S(2)}, u32[]{:S(2)}) collective-permute-start(bf16[8,128,128]{2,1,0:T(8,128)(2,1)} %get-tuple-element.9), channel_id=1, source_target_pairs={{4,0},{8,4},{12,8},{16,12},{20,16},{24,20},{28,24},{32,28},{36,32}... | collective-permute-start | bytes 786440 | tf_op jit(solution)/shard_map/ppermute | solution.py:31
  214.5 26.0 %all-to-all-start.4 = ((f32[64,1,1024]{2,1,0:T(1,128)}), f32[64,1,1024]{2,1,0:T(1,128)S(1)}, u32[]{:S(2)}, u32[]{:S(2)}) async-start(f32[64,1,1024]{2,1,0:T(1,128)} %broadcast_in_dim.21), calls=%async_computation.4 | async-start | bytes 524288 | tf_op jit(solution)/shard_map/all_to_all | solution.py:21
where the time goes:
time: 253 us; the launch traced here: 252 us
  starting transfers between devices  70 us (28%)
  waiting for transfers between devices  58.6 us (23%)
  other arithmetic  54 us (21%)
  local copies, waits for them, and re-layouts  38.8 us (15%)
  matrix products  17.7 us (7%)
  blocking collectives  11.8 us (5%)
    all_to_all x3, waiting for transfers between devices, from_everyone(): return lax.all_to_all(copies, axis, split_axis=0, concat_axis=0, tiled=True)  50.2 us
    scatter-add x2, other arithmetic, spread_tiles(): jax.ops.segment_sum(products.reshape(tile_count * count, tile_size, col_c...  40.5 us
    ppermute x8, starting transfers between devices, from_behind(): lax.ppermute(value, axis, [(source, source + steps) for source in range(i...  27.9 us
    all_to_all x3, starting transfers between devices, from_everyone(): return lax.all_to_all(copies, axis, split_axis=0, concat_axis=0, tiled=True)  22.8 us
    all_to_all x1, starting transfers between devices, sum_in_two_steps(): return jnp.sum(lax.all_to_all(own, far, 0, 0, tiled=True), axis=0)  19.3 us
    reshape x2, local copies, waits for them, and re-layouts, spread_tiles(): products.reshape(tile_count * count, tile_size, col_count)  13.1 us
    ppermute x8, waiting for transfers between devices, from_behind(): lax.ppermute(value, axis, [(source, source + steps) for source in range(i...  8.36 us
    another operation x3, other arithmetic  7.68 us
  transfers between devices with their start and end apart: 12, of which 6 were waited for; matrix products, arithmetic and copies ran while one was open for 19% of the time, Pallas kernels for 0%

commit v1 on v0

v1 whole, which is shorter than its diff:
```python
import functools
import math

import jax
import jax.numpy as jnp
from jax import lax
from jax.experimental import pallas as pl
from jax.experimental.pallas import tpu as pltpu
from jax.sharding import PartitionSpec as P

MESH = pl.DeviceIdType.MESH
BF = jnp.bfloat16
F32 = jnp.float32
IF, OF, IN, ON = 0, 1, 2, 3
H, B, N, A = 0, 1, 2, 3


def kernel(
    nz, ny, td, scale,
    gp2, agg2, w2, pre1, agg1, w1, blocks, ints, floats,
    gw2, gw1, gi,
    gath, blk, wv, pre, agg, aggt, prod, run, out, rec, giv, wacc, fin,
    w1s, w1r, wzs, wzr, wys, wyr, wgs, wgr, wcs, wcr,
    lsem, osem, gsend, grecv, ysend, yrecv, csend, crecv, zsend, zrecv, vsend, vrecv, tsend, trecv, c2send, c2recv,
):
    nb, tile, _ = blocks.shape
    bl = nb // td
    half = td // 2
    q = td // 4
    ch = q * tile
    yc, yt = 2, half // 2
    nx = lax.axis_size("feat")
    nd = lax.axis_size("dom")
    p = lax.axis_index("dom")
    x = lax.axis_index("feat")
    core = lax.rem(p, 2)
    y = lax.rem(p // 2, ny)
    z = p // (2 * ny)
    sig = 2 * core - 1

    def dom(step):
        return lax.rem(p + step + 2 * nd, nd)

    right = (p, lax.rem(x + 1, nx))
    left = (p, lax.rem(x + nx - 1, nx))
    partner, near, far, back = (dom(-sig), x), (dom(sig), x), (dom(2 * sig), x), (dom(-2 * sig), x)

    def zdev(k):
        return (k * (2 * ny) + y * 2 + core, x)

    def ydev(k):
        return (z * (2 * ny) + k * 2 + core, x)

    local = []

    def fetch(src, dst, i):
        cp = pltpu.make_async_copy(src, dst, lsem.at[i])
        cp.start()
        return cp

    def cols(k):
        return pl.ds(pl.multiple_of(k * tile, tile), tile)

    barrier = pltpu.get_barrier_semaphore()
    for dev in (left, right, partner, near, far, back):
        pl.semaphore_signal(barrier, inc=1, device_id=dev, device_id_type=MESH)

    def greet(k, _):
        pl.semaphore_signal(barrier, inc=1, device_id=zdev(lax.rem(z + k, nz)), device_id_type=MESH)
        return 0

    lax.fori_loop(1, nz, greet, 0)

    def greet_y(k, _):
        pl.semaphore_signal(barrier, inc=1, device_id=ydev(lax.rem(y + k, ny)), device_id_type=MESH)
        return 0

    lax.fori_loop(1, ny, greet_y, 0)

    own_cp = fetch(gp2, gath.at[0, :, cols(x)], 0)
    w2_cp = fetch(w2, wv.at[0], 1)
    agg2_cp = fetch(agg2, agg.at[0], 2)
    blk_cp = fetch(blocks, blk, 3)
    pre_cp = fetch(pre1, pre, 4)
    w1_cp = fetch(w1, wv.at[1], 5)
    agg1_cp = fetch(agg1, agg.at[1], 6)

    pl.semaphore_wait(barrier, 6 + nz - 1 + ny - 1)

    sends = []

    def remote(src, dst, ssem, rsem, dev):
        return pltpu.make_async_remote_copy(
            src_ref=src, dst_ref=dst, send_sem=ssem, recv_sem=rsem, device_id=dev, device_id_type=MESH
        )

    def send(*a):
        cp = remote(*a)
        cp.start()
        sends.append(cp)

    def first_tile(c):
        base = (1 - core) * half if c < 2 else core * half
        return base + (c % 2) * q

    def rows(c):
        return pl.ds(pl.multiple_of(first_tile(c) * tile, tile), ch)

    def gcopy(l, c, way, owner, dev):
        dst = gath.at[l, rows(c), cols(owner)]
        src = gp2.at[rows(c), :] if l == 0 and way < 2 else dst
        return src, dst, gsend.at[l, c, way], grecv.at[l, c, way], dev

    def send_own(l, c, way):
        send(*gcopy(l, c, way, x, right if way == 0 else left))

    def arrived(l, c, way):
        owner = lax.rem(x + (nx - 1, 1, 2)[way], nx)
        remote(*gcopy(l, c, way, owner, left)).wait_recv()

    def forward(l, c):
        if c % 2 == 0:
            arrived(l, c, 0)
            send(*gcopy(l, c, 2, left[1], right))
        else:
            arrived(l, c, 1)
            send(*gcopy(l, c, 2, right[1], left))

    def dense(l, c):
        arrived(l, c, 1 if c % 2 == 0 else 0)
        arrived(l, c, 2)

        def one(t, _):
            k = first_tile(c) + t
            g = gath[l, pl.ds(pl.multiple_of(k * tile, tile), tile), :]
            v = lax.dot_general(g, wv[l], (((1,), (1,)), ((), ())), preferred_element_type=F32).astype(BF)
            b = blk[pl.ds(k * bl, bl)].reshape(bl * tile, tile)
            prod[pl.ds(k * bl, bl)] = jnp.dot(b, v, preferred_element_type=F32).reshape(bl, tile, tile)
            return 0

        lax.fori_loop(0, q, one, 0)
        term = jnp.dot(aggt[l, c], gath[l, rows(c), :], preferred_element_type=F32)
        if c == 0:
            wacc[l] = term
        else:
            wacc[l] += term

    def transpose_agg(l):
        for c in range(4):
            aggt[l, c] = agg[l, rows(c), :].T

    def run_sums():
        def one(i, acc):
            acc = acc * floats[i] + prod[ints[i]]
            run[i] = acc
            return acc

        lax.fori_loop(0, nb, one, jnp.zeros((tile, tile), F32))

    def slot(s):
        return run[ints[nb + s]] * floats[nb + s]

    def ycopy(l, g, c, dev):
        at = pl.ds(c * yt, yt)
        return out.at[l, g, at], rec.at[l, g, at], ysend.at[l, g, c], yrecv.at[l, g, c], dev

    def emit(l, g, c, dev):
        def one(j, _):
            val = slot(g * half + c * yt + j)
            if g == ON:
                val = val + rec[l, H, c * yt + j].astype(F32)
            out[l, g, c * yt + j] = val.astype(BF)
            return 0

        if g == ON:
            remote(*ycopy(l, H, c, partner)).wait_recv()
        lax.fori_loop(0, yt, one, 0)
        send(*ycopy(l, g, c, dev))

    def spread(l):
        run_sums()
        for c in range(yc):
            emit(l, IF, c, partner)
        for c in range(yc):
            emit(l, OF, c, far)
        for c in range(yc):
            emit(l, IN, c, partner)
        for c in range(yc):
            emit(l, ON, c, near)

    def collect(l, c, put):
        groups = (B, N) if c < 2 else (A,)
        cc = c % 2
        for g in groups:
            remote(*ycopy(l, g, cc, partner)).wait_recv()

        def one(j, _):
            k = first_tile(c) + j
            val = slot(4 * half + k)
            for g in groups:
                val = val + rec[l, g, cc * yt + j].astype(F32)
            put(k, val)
            return 0

        lax.fori_loop(0, q, one, 0)

    hr = tile // 2
    rc = wzs.shape[1] // 2
    pr = hr // rc

    def piece(k):
        return pl.ds(pl.multiple_of((k // 2) * pr, pr), pr), pl.ds(pl.multiple_of(lax.rem(k, 2) * 256, 256), 256)

    def c1copy(l):
        return w1s.at[l], w1r.at[l], csend.at[l], crecv.at[l], partner

    def weight1(l):
        w1s[l] = (wacc[l, pl.ds(pl.multiple_of((1 - core) * hr, hr), hr), :] * scale).astype(BF)
        send(*c1copy(l))

    def others(n, me, make):
        def go(k, _):
            make(lax.rem(me + k, n)).start()
            return 0

        lax.fori_loop(1, n, go, 0)

    def all_recv(n, me, make):
        def go(k, _):
            make(lax.rem(me + k, n)).wait_recv()
            return 0

        lax.fori_loop(1, n, go, 0)

    def all_sent(n, me, make):
        def go(k, _):
            make(lax.rem(me + k, n)).wait_send()
            return 0

        lax.fori_loop(1, n, go, 0)

    def zout(l):
        return lambda k: remote(wzs.at[l, k], wzr.at[l, z], zsend.at[l, k], zrecv.at[l, z], zdev(k))

    def zin(l):
        return lambda k: remote(wzs.at[l, k], wzr.at[l, k], zsend.at[l, k], zrecv.at[l, k], zdev(k))

    def yout(l):
        return lambda k: remote(wys.at[l], wyr.at[l, y], vsend.at[l, k], vrecv.at[l, y], ydev(k))

    def yin(l):
        return lambda k: remote(wys.at[l], wyr.at[l, k], vsend.at[l, k], vrecv.at[l, k], ydev(k))

    def gout(l):
        return lambda k: remote(wgs.at[l], wgr.at[l, z], tsend.at[l, k], trecv.at[l, z], zdev(k))

    def gin(l):
        return lambda k: remote(wgs.at[l], wgr.at[l, k], tsend.at[l, k], trecv.at[l, k], zdev(k))

    def weight2(l):
        remote(*c1copy(l)).wait_recv()
        fin[l] = wacc[l, pl.ds(pl.multiple_of(core * hr, hr), hr), :] * scale + w1r[l].astype(F32)

        for k in range(nz):
            r, c = k // 2, k % 2
            wzs[l, k] = fin[l, r * pr:(r + 1) * pr, c * 256:(c + 1) * 256].astype(BF)
        others(nz, z, zout(l))

    def weight3(l):
        wzr[l, z] = wzs[l, z]
        all_recv(nz, z, zin(l))
        total = wzr[l, 0].astype(F32)
        for k in range(1, nz):
            total = total + wzr[l, k].astype(F32)
        wys[l] = total.astype(BF)
        others(ny, y, yout(l))

    def weight4(l):
        wyr[l, y] = wys[l]
        all_recv(ny, y, yin(l))
        total = wyr[l, 0].astype(F32)
        for k in range(1, ny):
            total = total + wyr[l, k].astype(F32)
        wgs[l] = total.astype(BF)
        others(nz, z, gout(l))

    def c2copy(l):
        return wcs.at[l], wcr.at[l], c2send.at[l], c2recv.at[l], partner

    def weight5(l):
        wgr[l, z] = wgs[l]
        all_recv(nz, z, gin(l))
        for k in range(nz):
            r, c = k // 2, k % 2
            wcs[l, r * pr:(r + 1) * pr, c * 256:(c + 1) * 256] = wgr[l, k]
        send(*c2copy(l))
        wacc[l, pl.ds(pl.multiple_of(core * hr, hr), hr), :] = wcs[l].astype(F32)

    outs = []

    def weight6(l):
        remote(*c2copy(l)).wait_recv()
        wacc[l, pl.ds(pl.multiple_of((1 - core) * hr, hr), hr), :] = wcr[l].astype(F32)
        cp = pltpu.make_async_copy(wacc.at[l], (gw2, gw1)[l], osem.at[l])
        cp.start()
        outs.append(cp)

    for c, d in ((0, 1), (2, 3), (1, 0), (3, 2)):
        send_own(0, c, 0)
        send_own(0, d, 1)
    agg2_cp.wait()
    transpose_agg(0)
    own_cp.wait()
    w2_cp.wait()
    forward(0, 0)
    forward(0, 1)
    blk_cp.wait()
    dense(0, 0)
    forward(0, 2)
    dense(0, 1)
    forward(0, 3)
    dense(0, 2)
    dense(0, 3)
    weight1(0)
    spread(0)
    weight2(0)
    pre_cp.wait()
    w1_cp.wait()

    def put_hidden(k, val):
        at = pl.ds(pl.multiple_of(k * tile, tile), tile)
        gath[1, at, cols(x)] = jnp.where(pre[at, :].astype(F32) > 0, val, 0.0).astype(BF)

    for c in range(4):
        collect(0, c, put_hidden)
        send_own(1, c, c % 2)
        send_own(1, c, 1 - c % 2)
        if c == 1:
            agg1_cp.wait()
            transpose_agg(1)
            forward(1, 0)
        if c == 2:
            forward(1, 1)
    weight3(0)
    dense(1, 0)
    forward(1, 2)
    weight4(0)
    dense(1, 1)
    forward(1, 3)
    weight5(0)
    dense(1, 2)
    weight6(0)
    dense(1, 3)
    weight1(1)
    spread(1)
    weight2(1)

    def put_input(k, val):
        giv[k] = val.astype(BF)

    for c in range(4):
        collect(1, c, put_input)
        at = pl.ds(first_tile(c), q)
        cp = pltpu.make_async_copy(giv.at[at], gi.at[at], osem.at[2 + c])
        cp.start()
        outs.append(cp)
        if c == 1:
            weight3(1)
        if c == 2:
            weight4(1)
    weight5(1)
    weight6(1)
    for cp in sends:
        cp.wait_send()
    for l in range(2):
        all_sent(nz, z, zin(l))
        all_sent(ny, y, yin(l))
        all_sent(nz, z, gin(l))
    for cp in outs:
        cp.wait()


def lists(targets, tile_count):
    p = lax.axis_index("dom")
    half = tile_count // 2
    sig = 2 * lax.rem(p, 2) - 1
    flat = targets.reshape(-1)
    nb = flat.shape[0]
    rel = flat - (p - 2) * tile_count
    off = (rel // tile_count - 2)
    at = rel % tile_count
    turned = off * sig
    group = jnp.where(turned == -2, IF, jnp.where(turned == 2, OF, jnp.where(turned == -1, IN, ON)))
    slot = jnp.where(off == 0, 4 * half + at, group * half + jnp.where(off < 0, at - half, at))
    idx = jnp.arange(nb, dtype=jnp.int32)
    key = slot * nb + idx
    rank = jnp.sum((key[None, :] < key[:, None]).astype(jnp.int32), axis=1)
    hit = rank[None, :] == idx[:, None]
    order = jnp.sum(jnp.where(hit, idx[None, :], 0), axis=1)
    prev = rank[None, :] == idx[:, None] - 1
    keep = jnp.sum(jnp.where(hit, slot[None, :], 0), axis=1) == jnp.sum(jnp.where(prev, slot[None, :] + 1, 0), axis=1) - 1
    slots = jnp.arange(4 * half + tile_count, dtype=jnp.int32)
    last = jnp.sum((slot[None, :] <= slots[:, None]).astype(jnp.int32), axis=1) - 1
    some = jnp.any(slot[None, :] == slots[:, None], axis=1)
    ints = jnp.concatenate([order, jnp.maximum(last, 0)])
    floats = jnp.concatenate([keep, some]).astype(F32)
    return ints, floats


def sizes(nd):
    chips = nd // 2
    nz = 1
    while nz * nz < chips:
        nz *= 2
    return nz, chips // nz


def shards(grad_pre2, aggregated2, weight2, pre1, aggregated1, weight1, blocks, targets):
    td, bl, tile, _ = blocks.shape
    nb, half, q = td * bl, td // 2, td // 4
    nd = lax.axis_size("dom")
    rows, d = grad_pre2.shape[0], weight2.shape[1]
    nz, ny = sizes(nd)
    scale = 1.0 / math.sqrt(rows * nd)
    ints, floats = lists(targets, td)
    pr = tile // 2 // max(1, nz // 2)
    hbm = pl.BlockSpec(memory_space=pl.ANY)
    smem = pl.BlockSpec(memory_space=pltpu.SMEM)
    dma = pltpu.SemaphoreType.DMA
    gw2, gw1, gi = pl.pallas_call(
        functools.partial(kernel, nz, ny, td, scale),
        out_shape=(
            jax.ShapeDtypeStruct((tile, d), F32),
            jax.ShapeDtypeStruct((tile, d), F32),
            jax.ShapeDtypeStruct((td, tile, tile), BF),
        ),
        in_specs=[hbm] * 7 + [smem] * 2,
        out_specs=(hbm, hbm, hbm),
        scratch_shapes=[
            pltpu.VMEM((2, rows, d), BF),
            pltpu.VMEM((nb, tile, tile), BF),
            pltpu.VMEM((2, tile, d), BF),
            pltpu.VMEM((rows, tile), BF),
            pltpu.VMEM((2, rows, tile), BF),
            pltpu.VMEM((2, 4, tile, rows // 4), BF),
            pltpu.VMEM((nb, tile, tile), F32),
            pltpu.VMEM((nb, tile, tile), F32),
            pltpu.VMEM((2, 4, half, tile, tile), BF),
            pltpu.VMEM((2, 4, half, tile, tile), BF),
            pltpu.VMEM((td, tile, tile), BF),
            pltpu.VMEM((2, tile, d), F32),
            pltpu.VMEM((2, tile // 2, d), F32),
            pltpu.VMEM((2, tile // 2, d), BF),
            pltpu.VMEM((2, tile // 2, d), BF),
            pltpu.VMEM((2, nz, pr, 256), BF),
            pltpu.VMEM((2, nz, pr, 256), BF),
            pltpu.VMEM((2, pr, 256), BF),
            pltpu.VMEM((2, ny, pr, 256), BF),
            pltpu.VMEM((2, pr, 256), BF),
            pltpu.VMEM((2, nz, pr, 256), BF),
            pltpu.VMEM((2, tile // 2, d), BF),
            pltpu.VMEM((2, tile // 2, d), BF),
            dma((7,)),
            dma((6,)),
            dma((2, 4, 3)),
            dma((2, 4, 3)),
            dma((2, 4, 2)),
            dma((2, 4, 2)),
            dma((2,)),
            dma((2,)),
            dma((2, nz)),
            dma((2, nz)),
            dma((2, ny)),
            dma((2, ny)),
            dma((2, nz)),
            dma((2, nz)),
            dma((2,)),
            dma((2,)),
        ],
        compiler_params=pltpu.CompilerParams(
            collective_id=0, has_side_effects=True, vmem_limit_bytes=48 * 1024 * 1024
        ),
    )(grad_pre2, aggregated2, weight2, pre1, aggregated1, weight1, blocks.reshape(nb, tile, tile), ints, floats)
    return gw2, gw1, gi.reshape(rows, tile)


def solution(mesh):
    placed = (
        P("dom", "feat"),
        P("dom", "feat"),
        P("feat", None),
        P("dom", "feat"),
        P("dom", "feat"),
        P("feat", None),
        P("dom", None, None, None),
        P("dom", None),
    )
    return jax.shard_map(
        shards,
        mesh=mesh,
        in_specs=placed,
        out_specs=(P("feat", None), P("feat", None), P("dom", "feat")),
        check_vma=False,
    )
```

time: 253 us -> 104 us (0.41)
  Pallas kernels: 0 us -> 93.4 us
  starting transfers between devices: 70 us -> 0 us
  waiting for transfers between devices: 58.6 us -> 0 us
  other arithmetic: 54 us -> 1.5 us
  local copies, waits for them, and re-layouts: 38.8 us -> 8.35 us
  matrix products: 17.7 us -> 0 us
  blocking collectives: 11.8 us -> 0 us
    pallas_call x0 -> x1, Pallas kernels: none -> 93.4 us  [shards(): pl.pallas_call(functools.partial(kernel, nz, ny, td, scale), out_shape=(j...]
    all_to_all x4 -> x0, waiting for transfers between devices: 50.2 us -> none  [the longest x3 50.2 us: from_everyone(): return lax.all_to_all(copies, axis, split_axis=0, concat_axis=0, tiled=True)]
    all_to_all x4 -> x0, starting transfers between devices: 42.1 us -> none  [the longest x3 22.8 us: from_everyone(): return lax.all_to_all(copies, axis, split_axis=0, concat_axis=0, tiled=True)]
    scatter-add x2 -> x0, other arithmetic: 40.5 us -> none  [spread_tiles(): jax.ops.segment_sum(products.reshape(tile_count * count, tile_size, col_c...]
    ppermute x8 -> x0, starting transfers between devices: 27.9 us -> none  [from_behind(): lax.ppermute(value, axis, [(source, source + steps) for source in range(i...]
    dot_general x6 -> x0, matrix products: 17.7 us -> none  [the longest x2 7.35 us: spread_tiles(): jnp.einsum('rkij,rjc->rkic', blocks, sources, preferred_element_type=jnp....]
    reshape x4 -> x0, local copies, waits for them, and re-layouts: 15 us -> none  [the longest x2 13.1 us: spread_tiles(): products.reshape(tile_count * count, tile_size, col_count)]
    all_to_all x2 -> x0, blocking collectives: 11.8 us -> none  [the longest x1 7.22 us: from_everyone(): return lax.all_to_all(copies, axis, split_axis=0, concat_axis=0, tiled=True)]
  transfers between devices with their start and end apart: 12 -> 0, of which waited for: 6 -> 0; matrix products, arithmetic and copies ran while one was open for 19% -> 0% of each run, Pallas kernels for 0% -> 0%
where the time goes in v1:
time: 104 us
  Pallas kernels  93.4 us (90%)
  local copies, waits for them, and re-layouts  8.35 us (8%)
  other arithmetic  1.5 us (1%)
    pallas_call x1, Pallas kernels, shards(): pl.pallas_call(functools.partial(kernel, nz, ny, td, scale), out_shape=(j...  93.4 us
    unnamed x15, local copies, waits for them, and re-layouts  8.18 us

profile of v1, /device:TPU:1, one launch (start us, length us, event | category | flops | bytes accessed | tf_op | source)
XLA Modules:
  0.0 103.9 jit_solution(257303089561797522)
XLA Ops:
  0.6 0.7 broadcast_subtract_fusion
  1.3 0.1 copy.13
  1.4 0.1 sub.56
  1.5 0.2 convert_reduce_fusion
  1.7 0.2 select_reduce_fusion
  1.9 0.1 convert_reduce_fusion.1
  2.1 0.1 fusion
  2.2 0.1 add_convert_fusion.floats
  2.3 0.1 pad_add_fusion.ints
  2.3 0.0 copy-start
  2.3 1.0 %copy-done = bf16[2048,128]{1,0:T(8,128)(2,1)S(1)} copy-done((bf16[2048,128]{1,0:T(8,128)(2,1)S(1)}, bf16[2048,128]{1,0:T(8,128)(2,1)}, u32[]{:S(2)}) %copy-start) | copy-done | bytes 524312
  3.4 0.0 copy-start.1
  3.4 1.0 %copy-done.1 = bf16[2048,128]{1,0:T(8,128)(2,1)S(1)} copy-done((bf16[2048,128]{1,0:T(8,128)(2,1)S(1)}, bf16[2048,128]{1,0:T(8,128)(2,1)}, u32[]{:S(2)}) %copy-start.1) | copy-done | bytes 524312
  4.4 0.0 copy-start.2
  4.4 1.0 %copy-done.2 = bf16[2048,128]{1,0:T(8,128)(2,1)S(1)} copy-done((bf16[2048,128]{1,0:T(8,128)(2,1)S(1)}, bf16[2048,128]{1,0:T(8,128)(2,1)}, u32[]{:S(2)}) %copy-start.2) | copy-done | bytes 524312
  5.5 0.0 copy-start.3
  5.5 1.0 %copy-done.3 = bf16[2048,128]{1,0:T(8,128)(2,1)S(1)} copy-done((bf16[2048,128]{1,0:T(8,128)(2,1)S(1)}, bf16[2048,128]{1,0:T(8,128)(2,1)}, u32[]{:S(2)}) %copy-start.3) | copy-done | bytes 524312
  6.5 0.0 copy-start.4
  6.5 0.9 copy-done.4
  7.4 0.0 copy-start.5
  7.4 0.9 copy-done.5
  8.3 93.4 %shard_map.103 = (f32[128,512]{1,0:T(8,128)S(1)}, f32[128,512]{1,0:T(8,128)S(1)}, bf16[16,128,128]{2,1,0:T(8,128)(2,1)S(1)}) custom-call(bf16[2048,128]{1,0:T(8,128)(2,1)S(1)} %copy-done, bf16[2048,128]{1,0:T(8,128)(2,1)S(1)} %copy-done.1, bf16[128,512]{1,0:T(8,128)(2,1)S(1)} %copy-done.4, bf16[2048,128]{1,0:T(8,128)(2,1)S(1)} %copy-done.2, ...), custom_call_target="tpu_custom_call" | custom-call | tf_op jit(solution)/shard_map/pallas_call | solution.py:430
  101.7 0.7 copy.17
  102.4 0.7 copy.18
  103.1 0.8 copy.19
  (4 shorter events, 0.0 us)
Async XLA Ops:
  2.3 1.1 %copy-start = (bf16[2048,128]{1,0:T(8,128)(2,1)S(1)}, bf16[2048,128]{1,0:T(8,128)(2,1)}, u32[]{:S(2)}) copy-start(bf16[2048,128]{1,0:T(8,128)(2,1)} %gp2.1) | copy-start | bytes 1572868
  3.4 1.0 %copy-start.1 = (bf16[2048,128]{1,0:T(8,128)(2,1)S(1)}, bf16[2048,128]{1,0:T(8,128)(2,1)}, u32[]{:S(2)}) copy-start(bf16[2048,128]{1,0:T(8,128)(2,1)} %agg2.1) | copy-start | bytes 1572868
  4.4 1.0 %copy-start.2 = (bf16[2048,128]{1,0:T(8,128)(2,1)S(1)}, bf16[2048,128]{1,0:T(8,128)(2,1)}, u32[]{:S(2)}) copy-start(bf16[2048,128]{1,0:T(8,128)(2,1)} %pre1.1) | copy-start | bytes 1572868
  5.5 1.0 %copy-start.3 = (bf16[2048,128]{1,0:T(8,128)(2,1)S(1)}, bf16[2048,128]{1,0:T(8,128)(2,1)}, u32[]{:S(2)}) copy-start(bf16[2048,128]{1,0:T(8,128)(2,1)} %agg1.1) | copy-start | bytes 1572868
  6.5 0.9 copy-start.4
  7.4 0.9 copy-start.5

commit v2 on v1

--- a/solution.py
+++ b/solution.py
@@ -17,10 +17,10 @@
 
 def kernel(
     nz, ny, td, scale,
-    gp2, agg2, w2, pre1, agg1, w1, blocks, ints, floats,
-    gw2, gw1, gi,
-    gath, blk, wv, pre, agg, aggt, prod, run, out, rec, giv, wacc, fin,
-    w1s, w1r, wzs, wzr, wys, wyr, wgs, wgr, wcs, wcr,
+    gp2, agg2, w2, pre1, agg1, w1, blocks, tg,
+    gw, gi,
+    gath, blk, wv, pre, agg, aggt, prod, run, out, rec, giv, wacc, keys, slots, icols, fcols, ints, floats,
+    w1s, w1r, wzs, wzr, wys, wyr, wgs, wgr, wcr,
     lsem, osem, gsend, grecv, ysend, yrecv, csend, crecv, zsend, zrecv, vsend, vrecv, tsend, trecv, c2send, c2recv,
 ):
     nb, tile, _ = blocks.shape
@@ -138,27 +138,64 @@
             prod[pl.ds(k * bl, bl)] = jnp.dot(b, v, preferred_element_type=F32).reshape(bl, tile, tile)
             return 0
 
-        lax.fori_loop(0, q, one, 0)
         term = jnp.dot(aggt[l, c], gath[l, rows(c), :], preferred_element_type=F32)
         if c == 0:
             wacc[l] = term
         else:
             wacc[l] += term
+        if c == 3 and l == 1:
+            weight1(l)
+        lax.fori_loop(0, q, one, 0, unroll=True)
 
     def transpose_agg(l):
         for c in range(4):
             aggt[l, c] = agg[l, rows(c), :].T
 
+    def make_lists():
+        lane = lax.broadcasted_iota(jnp.int32, (1, tile), 1)
+
+        def one(i, row):
+            rel = tg[i // bl, lax.rem(i, bl)] - (p - 2) * td
+            off = lax.div(rel, td) - 2
+            at = lax.rem(rel, td)
+            turned = off * sig
+            group = jnp.where(turned == -2, IF, jnp.where(turned == 2, OF, jnp.where(turned == -1, IN, ON)))
+            to = jnp.where(off == 0, 4 * half + at, group * half + jnp.where(off < 0, at - half, at))
+            key = to * nb + i
+            slots[pl.ds(i, 1), :] = jnp.full((1, tile), to, jnp.int32)
+            keys[pl.ds(i, 1), :] = jnp.full((1, tile), key, jnp.int32)
+            return jnp.where(lane == i, key, row)
+
+        row = lax.fori_loop(0, nb, one, jnp.full((1, tile), 1 << 20, jnp.int32))
+        place = lax.broadcasted_iota(jnp.int32, (nb, tile), 1)
+        block = lax.broadcasted_iota(jnp.int32, (nb, tile), 0)
+        rank = jnp.sum((row < keys[...]).astype(jnp.int32), axis=1, keepdims=True)
+
+        def add(mask, what):
+            return jnp.sum(jnp.where(mask, what, 0), axis=0, keepdims=True)
+
+        now, before = add(rank == place, slots[...]), add(rank == place - 1, slots[...])
+        icols[0:1, :] = add(rank == place, block)
+        icols[1:2, :] = jnp.maximum(add(slots[...] <= place, 1) - 1, 0)
+        fcols[0:1, :] = jnp.where((now == before) & (lane > 0), 1.0, 0.0)
+        fcols[1:2, :] = jnp.where(add(slots[...] == place, 1) > 0, 1.0, 0.0)
+        icp = pltpu.make_async_copy(icols, ints, lsem.at[7])
+        fcp = pltpu.make_async_copy(fcols, floats, lsem.at[8])
+        icp.start()
+        fcp.start()
+        icp.wait()
+        fcp.wait()
+
     def run_sums():
         def one(i, acc):
-            acc = acc * floats[i] + prod[ints[i]]
+            acc = acc * floats[0, i] + prod[ints[0, i]]
             run[i] = acc
             return acc
 
         lax.fori_loop(0, nb, one, jnp.zeros((tile, tile), F32))
 
     def slot(s):
-        return run[ints[nb + s]] * floats[nb + s]
+        return run[ints[1, s]] * floats[1, s]
 
     def ycopy(l, g, c, dev):
         at = pl.ds(c * yt, yt)
@@ -177,16 +214,17 @@
         lax.fori_loop(0, yt, one, 0)
         send(*ycopy(l, g, c, dev))
 
-    def spread(l):
+    def spread(l, between):
         run_sums()
         for c in range(yc):
             emit(l, IF, c, partner)
+        between(l)
         for c in range(yc):
             emit(l, OF, c, far)
         for c in range(yc):
+            emit(l, ON, c, near)
+        for c in range(yc):
             emit(l, IN, c, partner)
-        for c in range(yc):
-            emit(l, ON, c, near)
 
     def collect(l, c, put):
         groups = (B, N) if c < 2 else (A,)
@@ -204,18 +242,17 @@
 
         lax.fori_loop(0, q, one, 0)
 
-    hr = tile // 2
-    rc = wzs.shape[1] // 2
-    pr = hr // rc
-
-    def piece(k):
-        return pl.ds(pl.multiple_of((k // 2) * pr, pr), pr), pl.ds(pl.multiple_of(lax.rem(k, 2) * 256, 256), 256)
+    hc = wacc.shape[2] // 2
+
+    def half_of(l, h):
+        at = pl.ds(pl.multiple_of(h * hc, hc), hc)
+        return (wacc[l, :, at] * scale).reshape(wzs.shape[1:])
 
     def c1copy(l):
         return w1s.at[l], w1r.at[l], csend.at[l], crecv.at[l], partner
 
     def weight1(l):
-        w1s[l] = (wacc[l, pl.ds(pl.multiple_of((1 - core) * hr, hr), hr), :] * scale).astype(BF)
+        w1s[l] = half_of(l, 1 - core).astype(BF)
         send(*c1copy(l))
 
     def others(n, me, make):
@@ -239,75 +276,80 @@
 
         lax.fori_loop(1, n, go, 0)
 
+    side, at_a, at_b = nz, (z, y), (y, z)
+
+    def adev(l, k):
+        return zdev(k) if l == 0 else ydev(k)
+
+    def bdev(l, k):
+        return ydev(k) if l == 0 else zdev(k)
+
     def zout(l):
-        return lambda k: remote(wzs.at[l, k], wzr.at[l, z], zsend.at[l, k], zrecv.at[l, z], zdev(k))
+        return lambda k: remote(wzs.at[l, k], wzr.at[l, at_a[l]], zsend.at[l, k], zrecv.at[l, at_a[l]], adev(l, k))
 
     def zin(l):
-        return lambda k: remote(wzs.at[l, k], wzr.at[l, k], zsend.at[l, k], zrecv.at[l, k], zdev(k))
+        return lambda k: remote(wzs.at[l, k], wzr.at[l, k], zsend.at[l, k], zrecv.at[l, k], adev(l, k))
 
     def yout(l):
-        return lambda k: remote(wys.at[l], wyr.at[l, y], vsend.at[l, k], vrecv.at[l, y], ydev(k))
+        return lambda k: remote(wys.at[l], wyr.at[l, at_b[l]], vsend.at[l, k], vrecv.at[l, at_b[l]], bdev(l, k))
 
     def yin(l):
-        return lambda k: remote(wys.at[l], wyr.at[l, k], vsend.at[l, k], vrecv.at[l, k], ydev(k))
+        return lambda k: remote(wys.at[l], wyr.at[l, k], vsend.at[l, k], vrecv.at[l, k], bdev(l, k))
 
     def gout(l):
-        return lambda k: remote(wgs.at[l], wgr.at[l, z], tsend.at[l, k], trecv.at[l, z], zdev(k))
+        return lambda k: remote(wgs.at[l], wgr.at[l, at_a[l]], tsend.at[l, k], trecv.at[l, at_a[l]], adev(l, k))
 
     def gin(l):
-        return lambda k: remote(wgs.at[l], wgr.at[l, k], tsend.at[l, k], trecv.at[l, k], zdev(k))
+        return lambda k: remote(wgs.at[l], wgr.at[l, k], tsend.at[l, k], trecv.at[l, k], adev(l, k))
 
     def weight2(l):
         remote(*c1copy(l)).wait_recv()
-        fin[l] = wacc[l, pl.ds(pl.multiple_of(core * hr, hr), hr), :] * scale + w1r[l].astype(F32)
-
-        for k in range(nz):
-            r, c = k // 2, k % 2
-            wzs[l, k] = fin[l, r * pr:(r + 1) * pr, c * 256:(c + 1) * 256].astype(BF)
-        others(nz, z, zout(l))
+        wzs[l] = (half_of(l, core) + w1r[l].astype(F32)).astype(BF)
+        others(side, at_a[l], zout(l))
 
     def weight3(l):
-        wzr[l, z] = wzs[l, z]
-        all_recv(nz, z, zin(l))
+        wzr[l, at_a[l]] = wzs[l, at_a[l]]
+        all_recv(side, at_a[l], zin(l))
         total = wzr[l, 0].astype(F32)
         for k in range(1, nz):
             total = total + wzr[l, k].astype(F32)
         wys[l] = total.astype(BF)
-        others(ny, y, yout(l))
+        others(side, at_b[l], yout(l))
 
     def weight4(l):
-        wyr[l, y] = wys[l]
-        all_recv(ny, y, yin(l))
+        wyr[l, at_b[l]] = wys[l]
+        all_recv(side, at_b[l], yin(l))
         total = wyr[l, 0].astype(F32)
         for k in range(1, ny):
             total = total + wyr[l, k].astype(F32)
         wgs[l] = total.astype(BF)
-        others(nz, z, gout(l))
+        others(side, at_a[l], gout(l))
 
     def c2copy(l):
-        return wcs.at[l], wcr.at[l], c2send.at[l], c2recv.at[l], partner
+        return wgr.at[l], wcr.at[l], c2send.at[l], c2recv.at[l], partner
+
+    outs = []
+
+    def put_weight(l, h, src, i):
+        at = pl.ds(pl.multiple_of(h * hc, hc), hc)
+        cp = pltpu.make_async_copy(src.at[l], gw.at[l, :, :, at], osem.at[l, i])
+        cp.start()
+        outs.append(cp)
 
     def weight5(l):
-        wgr[l, z] = wgs[l]
-        all_recv(nz, z, gin(l))
-        for k in range(nz):
-            r, c = k // 2, k % 2
-            wcs[l, r * pr:(r + 1) * pr, c * 256:(c + 1) * 256] = wgr[l, k]
+        wgr[l, at_a[l]] = wgs[l]
+        all_recv(side, at_a[l], gin(l))
         send(*c2copy(l))
-        wacc[l, pl.ds(pl.multiple_of(core * hr, hr), hr), :] = wcs[l].astype(F32)
-
-    outs = []
+        put_weight(l, core, wgr, 0)
 
     def weight6(l):
         remote(*c2copy(l)).wait_recv()
-        wacc[l, pl.ds(pl.multiple_of((1 - core) * hr, hr), hr), :] = wcr[l].astype(F32)
-        cp = pltpu.make_async_copy(wacc.at[l], (gw2, gw1)[l], osem.at[l])
-        cp.start()
-        outs.append(cp)
+        put_weight(l, 1 - core, wcr, 1)
 
     for c, d in ((0, 1), (2, 3), (1, 0), (3, 2)):
         send_own(0, c, 0)
         send_own(0, d, 1)
+    make_lists()
     agg2_cp.wait()
     transpose_agg(0)
     own_cp.wait()
@@ -322,7 +364,7 @@
     dense(0, 2)
     dense(0, 3)
     weight1(0)
-    spread(0)
+    spread(0, lambda l: None)
     weight2(0)
     pre_cp.wait()
     w1_cp.wait()
@@ -351,9 +393,8 @@
     dense(1, 2)
     weight6(0)
     dense(1, 3)
-    weight1(1)
-    spread(1)
-    weight2(1)
+    spread(1, weight2)
+    weight3(1)
 
     def put_input(k, val):
         giv[k] = val.astype(BF)
@@ -361,50 +402,21 @@
     for c in range(4):
         collect(1, c, put_input)
         at = pl.ds(first_tile(c), q)
-        cp = pltpu.make_async_copy(giv.at[at], gi.at[at], osem.at[2 + c])
+        cp = pltpu.make_async_copy(giv.at[at], gi.at[at], osem.at[2 + c // 2, c % 2])
         cp.start()
         outs.append(cp)
         if c == 1:
-            weight3(1)
-        if c == 2:
             weight4(1)
     weight5(1)
     weight6(1)
     for cp in sends:
         cp.wait_send()
     for l in range(2):
-        all_sent(nz, z, zin(l))
-        all_sent(ny, y, yin(l))
-        all_sent(nz, z, gin(l))
+        all_sent(side, at_a[l], zin(l))
+        all_sent(side, at_b[l], yin(l))
+        all_sent(side, at_a[l], gin(l))
     for cp in outs:
         cp.wait()
-
-
-def lists(targets, tile_count):
-    p = lax.axis_index("dom")
-    half = tile_count // 2
-    sig = 2 * lax.rem(p, 2) - 1
-    flat = targets.reshape(-1)
-    nb = flat.shape[0]
-    rel = flat - (p - 2) * tile_count
-    off = (rel // tile_count - 2)
-    at = rel % tile_count
-    turned = off * sig
-    group = jnp.where(turned == -2, IF, jnp.where(turned == 2, OF, jnp.where(turned == -1, IN, ON)))
-    slot = jnp.where(off == 0, 4 * half + at, group * half + jnp.where(off < 0, at - half, at))
-    idx = jnp.arange(nb, dtype=jnp.int32)
-    key = slot * nb + idx
-    rank = jnp.sum((key[None, :] < key[:, None]).astype(jnp.int32), axis=1)
-    hit = rank[None, :] == idx[:, None]
-    order = jnp.sum(jnp.where(hit, idx[None, :], 0), axis=1)
-    prev = rank[None, :] == idx[:, None] - 1
-    keep = jnp.sum(jnp.where(hit, slot[None, :], 0), axis=1) == jnp.sum(jnp.where(prev, slot[None, :] + 1, 0), axis=1) - 1
-    slots = jnp.arange(4 * half + tile_count, dtype=jnp.int32)
-    last = jnp.sum((slot[None, :] <= slots[:, None]).astype(jnp.int32), axis=1) - 1
-    some = jnp.any(slot[None, :] == slots[:, None], axis=1)
-    ints = jnp.concatenate([order, jnp.maximum(last, 0)])
-    floats = jnp.concatenate([keep, some]).astype(F32)
-    return ints, floats
 
 
 def sizes(nd):
@@ -422,20 +434,19 @@
     rows, d = grad_pre2.shape[0], weight2.shape[1]
     nz, ny = sizes(nd)
     scale = 1.0 / math.sqrt(rows * nd)
-    ints, floats = lists(targets, td)
-    pr = tile // 2 // max(1, nz // 2)
-    hbm = pl.BlockSpec(memory_space=pl.ANY)
+    pr = tile // nz
+    hbm = pl.BlockSpec(memory_space=pltpu.HBM)
+    anywhere = pl.BlockSpec(memory_space=pl.ANY)
     smem = pl.BlockSpec(memory_space=pltpu.SMEM)
     dma = pltpu.SemaphoreType.DMA
-    gw2, gw1, gi = pl.pallas_call(
+    gw, gi = pl.pallas_call(
         functools.partial(kernel, nz, ny, td, scale),
         out_shape=(
-            jax.ShapeDtypeStruct((tile, d), F32),
-            jax.ShapeDtypeStruct((tile, d), F32),
+            jax.ShapeDtypeStruct((2, nz, pr, d), BF),
             jax.ShapeDtypeStruct((td, tile, tile), BF),
         ),
-        in_specs=[hbm] * 7 + [smem] * 2,
-        out_specs=(hbm, hbm, hbm),
+        in_specs=[hbm] * 7 + [smem],
+        out_specs=(anywhere, anywhere),
         scratch_shapes=[
             pltpu.VMEM((2, rows, d), BF),
             pltpu.VMEM((nb, tile, tile), BF),
@@ -449,19 +460,23 @@
             pltpu.VMEM((2, 4, half, tile, tile), BF),
             pltpu.VMEM((td, tile, tile), BF),
             pltpu.VMEM((2, tile, d), F32),
-            pltpu.VMEM((2, tile // 2, d), F32),
-            pltpu.VMEM((2, tile // 2, d), BF),
-            pltpu.VMEM((2, tile // 2, d), BF),
-            pltpu.VMEM((2, nz, pr, 256), BF),
-            pltpu.VMEM((2, nz, pr, 256), BF),
-            pltpu.VMEM((2, pr, 256), BF),
-            pltpu.VMEM((2, ny, pr, 256), BF),
-            pltpu.VMEM((2, pr, 256), BF),
-            pltpu.VMEM((2, nz, pr, 256), BF),
-            pltpu.VMEM((2, tile // 2, d), BF),
-            pltpu.VMEM((2, tile // 2, d), BF),
-            dma((7,)),
-            dma((6,)),
+            pltpu.VMEM((nb, tile), jnp.int32),
+            pltpu.VMEM((nb, tile), jnp.int32),
+            pltpu.VMEM((8, tile), jnp.int32),
+            pltpu.VMEM((8, tile), F32),
+            pltpu.SMEM((8, tile), jnp.int32),
+            pltpu.SMEM((8, tile), F32),
+            pltpu.VMEM((2, nz, pr, d // 2), BF),
+            pltpu.VMEM((2, nz, pr, d // 2), BF),
+            pltpu.VMEM((2, nz, pr, d // 2), BF),
+            pltpu.VMEM((2, nz, pr, d // 2), BF),
+            pltpu.VMEM((2, pr, d // 2), BF),
+            pltpu.VMEM((2, ny, pr, d // 2), BF),
+            pltpu.VMEM((2, pr, d // 2), BF),
+            pltpu.VMEM((2, nz, pr, d // 2), BF),
+            pltpu.VMEM((2, nz, pr, d // 2), BF),
+            dma((9,)),
+            dma((4, 2)),
             dma((2, 4, 3)),
             dma((2, 4, 3)),
             dma((2, 4, 2)),
@@ -478,10 +493,11 @@
             dma((2,)),
         ],
         compiler_params=pltpu.CompilerParams(
-            collective_id=0, has_side_effects=True, vmem_limit_bytes=48 * 1024 * 1024
+            collective_id=0, has_side_effects=True, vmem_limit_bytes=40 * 1024 * 1024
         ),
-    )(grad_pre2, aggregated2, weight2, pre1, aggregated1, weight1, blocks.reshape(nb, tile, tile), ints, floats)
-    return gw2, gw1, gi.reshape(rows, tile)
+    )(*(pltpu.with_memory_space_constraint(a, pltpu.HBM) for a in (grad_pre2, aggregated2, weight2, pre1, aggregated1, weight1, blocks.reshape(nb, tile, tile))), targets)
+    gw = gw.reshape(2, tile, d)
+    return gw[0].astype(F32), gw[1].astype(F32), gi.reshape(rows, tile)
 
 
 def solution(mesh):

time: 104 us -> 90 us (0.87)
  local copies, waits for them, and re-layouts: 8.35 us -> 1.58 us
  Pallas kernels: 93.4 us -> 86.8 us
    pallas_call x1, Pallas kernels: 93.4 us -> 86.8 us  [shards(): pl.pallas_call(functools.partial(kernel, nz, ny, td, scale), out_shape=(j...]
    unnamed x15 -> x2, local copies, waits for them, and re-layouts: 8.18 us -> 1.56 us
where the time goes in v2:
time: 90 us; the launch traced here: 89.9 us
  Pallas kernels  86.8 us (96%)
  local copies, waits for them, and re-layouts  1.58 us (2%)
    pallas_call x1, Pallas kernels, shards(): pl.pallas_call(functools.partial(kernel, nz, ny, td, scale), out_shape=(j...  86.8 us

profile of v2, /device:TPU:1, one launch (start us, length us, event | category | flops | bytes accessed | tf_op | source)
XLA Modules:
  0.0 89.9 jit_solution(13915001913548837122)
XLA Ops:
  0.6 0.8 copy.11.tg
  1.4 86.8 %shard_map.103 = (bf16[2,8,16,512]{3,2,1,0:T(8,128)(2,1)S(1)}, bf16[16,128,128]{2,1,0:T(8,128)(2,1)S(1)}) custom-call(bf16[2048,128]{1,0:T(8,128)(2,1)} %gp2.1, bf16[2048,128]{1,0:T(8,128)(2,1)} %agg2.1, bf16[128,512]{1,0:T(8,128)(2,1)} %w2.1, bf16[2048,128]{1,0:T(8,128)(2,1)} %pre1.1, bf16[2048,128]{1,0:T(8,128)(2,1)} %agg1.1, bf16[128,512]{1,0:T(8,128)(2,1)} %w1.1, ...), custom_call_target="tpu_custom_call" | custom-call | tf_op jit(solution)/shard_map/pallas_call | solution.py:442
  88.2 0.9 bitcast_convert_fusion
  89.1 0.8 copy.13
  (1 shorter events, 0.0 us)

commit v3 on v2

--- a/solution.py
+++ b/solution.py
@@ -9,6 +9,7 @@
 from jax.sharding import PartitionSpec as P
 
 MESH = pl.DeviceIdType.MESH
+PARTS = 2
 BF = jnp.bfloat16
 F32 = jnp.float32
 IF, OF, IN, ON = 0, 1, 2, 3
@@ -21,14 +22,15 @@
     gw, gi,
     gath, blk, wv, pre, agg, aggt, prod, run, out, rec, giv, wacc, keys, slots, icols, fcols, ints, floats,
     w1s, w1r, wzs, wzr, wys, wyr, wgs, wgr, wcr,
-    lsem, osem, gsend, grecv, ysend, yrecv, csend, crecv, zsend, zrecv, vsend, vrecv, tsend, trecv, c2send, c2recv,
+    lsem, osem, gisem, gsend, grecv, ysend, yrecv, csend, crecv, zsend, zrecv, vsend, vrecv, tsend, trecv, c2send, c2recv,
 ):
     nb, tile, _ = blocks.shape
     bl = nb // td
     half = td // 2
-    q = td // 4
+    q = half // PARTS
     ch = q * tile
-    yc, yt = 2, half // 2
+    chunks = 2 * PARTS
+    yc, yt = PARTS, q
     nx = lax.axis_size("feat")
     nd = lax.axis_size("dom")
     p = lax.axis_index("dom")
@@ -100,8 +102,8 @@
         sends.append(cp)
 
     def first_tile(c):
-        base = (1 - core) * half if c < 2 else core * half
-        return base + (c % 2) * q
+        base = (1 - core) * half if c < PARTS else core * half
+        return base + (c % PARTS) * q
 
     def rows(c):
         return pl.ds(pl.multiple_of(first_tile(c) * tile, tile), ch)
@@ -143,12 +145,12 @@
             wacc[l] = term
         else:
             wacc[l] += term
-        if c == 3 and l == 1:
+        if c == chunks - 1 and l == 1:
             weight1(l)
         lax.fori_loop(0, q, one, 0, unroll=True)
 
     def transpose_agg(l):
-        for c in range(4):
+        for c in range(chunks):
             aggt[l, c] = agg[l, rows(c), :].T
 
     def make_lists():
@@ -227,8 +229,8 @@
             emit(l, IN, c, partner)
 
     def collect(l, c, put):
-        groups = (B, N) if c < 2 else (A,)
-        cc = c % 2
+        groups = (B, N) if c < PARTS else (A,)
+        cc = c % PARTS
         for g in groups:
             remote(*ycopy(l, g, cc, partner)).wait_recv()
 
@@ -346,7 +348,8 @@
         remote(*c2copy(l)).wait_recv()
         put_weight(l, 1 - core, wcr, 1)
 
-    for c, d in ((0, 1), (2, 3), (1, 0), (3, 2)):
+    evens, odds = list(range(0, chunks, 2)), list(range(1, chunks, 2))
+    for c, d in zip(evens + odds, odds + evens):
         send_own(0, c, 0)
         send_own(0, d, 1)
     make_lists()
@@ -354,18 +357,16 @@
     transpose_agg(0)
     own_cp.wait()
     w2_cp.wait()
-    forward(0, 0)
-    forward(0, 1)
     blk_cp.wait()
-    dense(0, 0)
-    forward(0, 2)
-    dense(0, 1)
-    forward(0, 3)
-    dense(0, 2)
-    dense(0, 3)
+    for c in range(chunks):
+        forward(0, c)
+    for c in range(chunks):
+        dense(0, c)
     weight1(0)
     spread(0, lambda l: None)
     weight2(0)
+    agg1_cp.wait()
+    transpose_agg(1)
     pre_cp.wait()
     w1_cp.wait()
 
@@ -373,40 +374,33 @@
         at = pl.ds(pl.multiple_of(k * tile, tile), tile)
         gath[1, at, cols(x)] = jnp.where(pre[at, :].astype(F32) > 0, val, 0.0).astype(BF)
 
-    for c in range(4):
+    for c in range(chunks):
         collect(0, c, put_hidden)
         send_own(1, c, c % 2)
         send_own(1, c, 1 - c % 2)
-        if c == 1:
-            agg1_cp.wait()
-            transpose_agg(1)
-            forward(1, 0)
-        if c == 2:
-            forward(1, 1)
     weight3(0)
-    dense(1, 0)
-    forward(1, 2)
+    for c in range(chunks):
+        forward(1, c)
     weight4(0)
-    dense(1, 1)
-    forward(1, 3)
+    for c in range(chunks):
+        dense(1, c)
+    weight2(1)
+    spread(1, lambda l: None)
+    weight3(1)
     weight5(0)
-    dense(1, 2)
-    weight6(0)
-    dense(1, 3)
-    spread(1, weight2)
-    weight3(1)
 
     def put_input(k, val):
         giv[k] = val.astype(BF)
 
-    for c in range(4):
+    for c in range(chunks):
         collect(1, c, put_input)
         at = pl.ds(first_tile(c), q)
-        cp = pltpu.make_async_copy(giv.at[at], gi.at[at], osem.at[2 + c // 2, c % 2])
+        cp = pltpu.make_async_copy(giv.at[at], gi.at[at], gisem.at[c])
         cp.start()
         outs.append(cp)
-        if c == 1:
+        if c == PARTS - 1:
             weight4(1)
+    weight6(0)
     weight5(1)
     weight6(1)
     for cp in sends:
@@ -429,7 +423,7 @@
 
 def shards(grad_pre2, aggregated2, weight2, pre1, aggregated1, weight1, blocks, targets):
     td, bl, tile, _ = blocks.shape
-    nb, half, q = td * bl, td // 2, td // 4
+    nb, half = td * bl, td // 2
     nd = lax.axis_size("dom")
     rows, d = grad_pre2.shape[0], weight2.shape[1]
     nz, ny = sizes(nd)
@@ -453,7 +447,7 @@
             pltpu.VMEM((2, tile, d), BF),
             pltpu.VMEM((rows, tile), BF),
             pltpu.VMEM((2, rows, tile), BF),
-            pltpu.VMEM((2, 4, tile, rows // 4), BF),
+            pltpu.VMEM((2, 2 * PARTS, tile, rows // (2 * PARTS)), BF),
             pltpu.VMEM((nb, tile, tile), F32),
             pltpu.VMEM((nb, tile, tile), F32),
             pltpu.VMEM((2, 4, half, tile, tile), BF),
@@ -476,11 +470,12 @@
             pltpu.VMEM((2, nz, pr, d // 2), BF),
             pltpu.VMEM((2, nz, pr, d // 2), BF),
             dma((9,)),
-            dma((4, 2)),
-            dma((2, 4, 3)),
-            dma((2, 4, 3)),
-            dma((2, 4, 2)),
-            dma((2, 4, 2)),
+            dma((2, 2)),
+            dma((2 * PARTS,)),
+            dma((2, 2 * PARTS, 3)),
+            dma((2, 2 * PARTS, 3)),
+            dma((2, 4, PARTS)),
+            dma((2, 4, PARTS)),
             dma((2,)),
             dma((2,)),
             dma((2, nz)),

time: 90 us -> 84.6 us (0.940)
  Pallas kernels: 86.8 us -> 81.3 us
    pallas_call x1, Pallas kernels: 86.8 us -> 81.3 us  [shards(): pl.pallas_call(functools.partial(kernel, nz, ny, td, scale), out_shape=(j...]
where the time goes in v3:
time: 84.6 us; the launch traced here: 84.4 us
  Pallas kernels  81.3 us (96%)
  local copies, waits for them, and re-layouts  1.58 us (2%)
  other arithmetic  0.87 us (1%)
    pallas_call x1, Pallas kernels, shards(): pl.pallas_call(functools.partial(kernel, nz, ny, td, scale), out_shape=(j...  81.3 us

profile of v3, /device:TPU:1, one launch (start us, length us, event | category | flops | bytes accessed | tf_op | source)
XLA Modules:
  0.0 84.4 jit_solution(15584986107328751165)
XLA Ops:
  0.6 0.8 copy.11.tg
  1.4 81.3 %shard_map.103 = (bf16[2,8,16,512]{3,2,1,0:T(8,128)(2,1)S(1)}, bf16[16,128,128]{2,1,0:T(8,128)(2,1)S(1)}) custom-call(bf16[2048,128]{1,0:T(8,128)(2,1)} %gp2.1, bf16[2048,128]{1,0:T(8,128)(2,1)} %agg2.1, bf16[128,512]{1,0:T(8,128)(2,1)} %w2.1, bf16[2048,128]{1,0:T(8,128)(2,1)} %pre1.1, bf16[2048,128]{1,0:T(8,128)(2,1)} %agg1.1, bf16[128,512]{1,0:T(8,128)(2,1)} %w1.1, ...), custom_call_target="tpu_custom_call" | custom-call | tf_op jit(solution)/shard_map/pallas_call | solution.py:436
  82.8 0.9 %bitcast_convert_fusion = (f32[128,512]{1,0:T(8,128)}, f32[128,512]{1,0:T(8,128)}) fusion(bf16[1,8,16,512]{3,2,1,0:T(8,128)(2,1)S(1)} %get-tuple-element.7, bf16[1,8,16,512]{3,2,1,0:T(8,128)(2,1)S(1)} %get-tuple-element.8), kind=kLoop, calls=%fused_computation | loop fusion | flops 131072 | bytes 786432 | tf_op jit(solution)/shard_map/convert_element_type | solution.py:495
  83.6 0.8 copy.13
  (1 shorter events, 0.0 us)

commit v4 on v3

--- a/solution.py
+++ b/solution.py
@@ -9,7 +9,7 @@
 from jax.sharding import PartitionSpec as P
 
 MESH = pl.DeviceIdType.MESH
-PARTS = 2
+PARTS = 4
 BF = jnp.bfloat16
 F32 = jnp.float32
 IF, OF, IN, ON = 0, 1, 2, 3
@@ -18,9 +18,9 @@
 
 def kernel(
     nz, ny, td, scale,
-    gp2, agg2, w2, pre1, agg1, w1, blocks, tg,
+    gp2, agg2, w2, pre1, agg1, w1, blocks, targets,
     gw, gi,
-    gath, blk, wv, pre, agg, aggt, prod, run, out, rec, giv, wacc, keys, slots, icols, fcols, ints, floats,
+    gath, blk, wv, pre, agg, aggt, prod, run, out, rec, giv, wacc, keys, slots, icols, fcols, tg, ints, floats,
     w1s, w1r, wzs, wzr, wys, wyr, wgs, wgr, wcr,
     lsem, osem, gisem, gsend, grecv, ysend, yrecv, csend, crecv, zsend, zrecv, vsend, vrecv, tsend, trecv, c2send, c2recv,
 ):
@@ -79,6 +79,7 @@
 
     lax.fori_loop(1, ny, greet_y, 0)
 
+    tg_cp = fetch(targets, tg, 9)
     own_cp = fetch(gp2, gath.at[0, :, cols(x)], 0)
     w2_cp = fetch(w2, wv.at[0], 1)
     agg2_cp = fetch(agg2, agg.at[0], 2)
@@ -128,10 +129,16 @@
             arrived(l, c, 1)
             send(*gcopy(l, c, 2, right[1], left))
 
-    def dense(l, c):
+    def weigh(l, c):
         arrived(l, c, 1 if c % 2 == 0 else 0)
         arrived(l, c, 2)
-
+        term = jnp.dot(aggt[l, c], gath[l, rows(c), :], preferred_element_type=F32)
+        if c == 0:
+            wacc[l] = term
+        else:
+            wacc[l] += term
+
+    def multiply(l, c):
         def one(t, _):
             k = first_tile(c) + t
             g = gath[l, pl.ds(pl.multiple_of(k * tile, tile), tile), :]
@@ -140,13 +147,6 @@
             prod[pl.ds(k * bl, bl)] = jnp.dot(b, v, preferred_element_type=F32).reshape(bl, tile, tile)
             return 0
 
-        term = jnp.dot(aggt[l, c], gath[l, rows(c), :], preferred_element_type=F32)
-        if c == 0:
-            wacc[l] = term
-        else:
-            wacc[l] += term
-        if c == chunks - 1 and l == 1:
-            weight1(l)
         lax.fori_loop(0, q, one, 0, unroll=True)
 
     def transpose_agg(l):
@@ -155,9 +155,10 @@
 
     def make_lists():
         lane = lax.broadcasted_iota(jnp.int32, (1, tile), 1)
+        tg_cp.wait()
 
         def one(i, row):
-            rel = tg[i // bl, lax.rem(i, bl)] - (p - 2) * td
+            rel = tg[lax.rem(i, bl), i // bl] - (p - 2) * td
             off = lax.div(rel, td) - 2
             at = lax.rem(rel, td)
             turned = off * sig
@@ -216,17 +217,15 @@
         lax.fori_loop(0, yt, one, 0)
         send(*ycopy(l, g, c, dev))
 
-    def spread(l, between):
+    def spread(l):
         run_sums()
         for c in range(yc):
+            emit(l, OF, c, far)
             emit(l, IF, c, partner)
-        between(l)
         for c in range(yc):
-            emit(l, OF, c, far)
+            emit(l, IN, c, partner)
         for c in range(yc):
             emit(l, ON, c, near)
-        for c in range(yc):
-            emit(l, IN, c, partner)
 
     def collect(l, c, put):
         groups = (B, N) if c < PARTS else (A,)
@@ -286,6 +285,10 @@
     def bdev(l, k):
         return ydev(k) if l == 0 else zdev(k)
 
+    def piece(k):
+        n = wgs.shape[1]
+        return pl.ds(pl.multiple_of(k * n, n), n)
+
     def zout(l):
         return lambda k: remote(wzs.at[l, k], wzr.at[l, at_a[l]], zsend.at[l, k], zrecv.at[l, at_a[l]], adev(l, k))
 
@@ -299,10 +302,10 @@
         return lambda k: remote(wys.at[l], wyr.at[l, k], vsend.at[l, k], vrecv.at[l, k], bdev(l, k))
 
     def gout(l):
-        return lambda k: remote(wgs.at[l], wgr.at[l, at_a[l]], tsend.at[l, k], trecv.at[l, at_a[l]], adev(l, k))
+        return lambda k: remote(wgs.at[l], wgr.at[l, piece(at_a[l])], tsend.at[l, k], trecv.at[l, at_a[l]], adev(l, k))
 
     def gin(l):
-        return lambda k: remote(wgs.at[l], wgr.at[l, k], tsend.at[l, k], trecv.at[l, k], adev(l, k))
+        return lambda k: remote(wgs.at[l], wgr.at[l, piece(k)], tsend.at[l, k], trecv.at[l, k], adev(l, k))
 
     def weight2(l):
         remote(*c1copy(l)).wait_recv()
@@ -334,12 +337,12 @@
 
     def put_weight(l, h, src, i):
         at = pl.ds(pl.multiple_of(h * hc, hc), hc)
-        cp = pltpu.make_async_copy(src.at[l], gw.at[l, :, :, at], osem.at[l, i])
+        cp = pltpu.make_async_copy(src.at[l], gw.at[l, :, at], osem.at[l, i])
         cp.start()
         outs.append(cp)
 
     def weight5(l):
-        wgr[l, at_a[l]] = wgs[l]
+        wgr[l, piece(at_a[l])] = wgs[l]
         all_recv(side, at_a[l], gin(l))
         send(*c2copy(l))
         put_weight(l, core, wgr, 0)
@@ -361,9 +364,10 @@
     for c in range(chunks):
         forward(0, c)
     for c in range(chunks):
-        dense(0, c)
+        weigh(0, c)
+        multiply(0, c)
     weight1(0)
-    spread(0, lambda l: None)
+    spread(0)
     weight2(0)
     agg1_cp.wait()
     transpose_agg(1)
@@ -382,10 +386,16 @@
     for c in range(chunks):
         forward(1, c)
     weight4(0)
-    for c in range(chunks):
-        dense(1, c)
+    for c in range(chunks - 2):
+        weigh(1, c)
+        multiply(1, c)
+    for c in range(chunks - 2, chunks):
+        weigh(1, c)
+    weight1(1)
+    for c in range(chunks - 2, chunks):
+        multiply(1, c)
     weight2(1)
-    spread(1, lambda l: None)
+    spread(1)
     weight3(1)
     weight5(0)
 
@@ -401,14 +411,18 @@
         if c == PARTS - 1:
             weight4(1)
     weight6(0)
-    weight5(1)
-    weight6(1)
     for cp in sends:
         cp.wait_send()
+    sends.clear()
     for l in range(2):
         all_sent(side, at_a[l], zin(l))
         all_sent(side, at_b[l], yin(l))
-        all_sent(side, at_a[l], gin(l))
+    all_sent(side, at_a[0], gin(0))
+    weight5(1)
+    weight6(1)
+    all_sent(side, at_a[1], gin(1))
+    for cp in sends:
+        cp.wait_send()
     for cp in outs:
         cp.wait()
 
@@ -431,15 +445,14 @@
     pr = tile // nz
     hbm = pl.BlockSpec(memory_space=pltpu.HBM)
     anywhere = pl.BlockSpec(memory_space=pl.ANY)
-    smem = pl.BlockSpec(memory_space=pltpu.SMEM)
     dma = pltpu.SemaphoreType.DMA
     gw, gi = pl.pallas_call(
         functools.partial(kernel, nz, ny, td, scale),
         out_shape=(
-            jax.ShapeDtypeStruct((2, nz, pr, d), BF),
+            jax.ShapeDtypeStruct((2, tile, d), BF),
             jax.ShapeDtypeStruct((td, tile, tile), BF),
         ),
-        in_specs=[hbm] * 7 + [smem],
+        in_specs=[hbm] * 8,
         out_specs=(anywhere, anywhere),
         scratch_shapes=[
             pltpu.VMEM((2, rows, d), BF),
@@ -458,6 +471,7 @@
             pltpu.VMEM((nb, tile), jnp.int32),
             pltpu.VMEM((8, tile), jnp.int32),
             pltpu.VMEM((8, tile), F32),
+            pltpu.SMEM((bl, td), jnp.int32),
             pltpu.SMEM((8, tile), jnp.int32),
             pltpu.SMEM((8, tile), F32),
             pltpu.VMEM((2, nz, pr, d // 2), BF),
@@ -467,9 +481,9 @@
             pltpu.VMEM((2, pr, d // 2), BF),
             pltpu.VMEM((2, ny, pr, d // 2), BF),
             pltpu.VMEM((2, pr, d // 2), BF),
-            pltpu.VMEM((2, nz, pr, d // 2), BF),
-            pltpu.VMEM((2, nz, pr, d // 2), BF),
-            dma((9,)),
+            pltpu.VMEM((2, tile, d // 2), BF),
+            pltpu.VMEM((2, tile, d // 2), BF),
+            dma((10,)),
             dma((2, 2)),
             dma((2 * PARTS,)),
             dma((2, 2 * PARTS, 3)),
@@ -490,8 +504,7 @@
         compiler_params=pltpu.CompilerParams(
             collective_id=0, has_side_effects=True, vmem_limit_bytes=40 * 1024 * 1024
         ),
-    )(*(pltpu.with_memory_space_constraint(a, pltpu.HBM) for a in (grad_pre2, aggregated2, weight2, pre1, aggregated1, weight1, blocks.reshape(nb, tile, tile))), targets)
-    gw = gw.reshape(2, tile, d)
+    )(*(pltpu.with_memory_space_constraint(a, pltpu.HBM) for a in (grad_pre2, aggregated2, weight2, pre1, aggregated1, weight1, blocks.reshape(nb, tile, tile), targets.T)))
     return gw[0].astype(F32), gw[1].astype(F32), gi.reshape(rows, tile)
 
 

time: 84.6 us -> 80.9 us (0.956)
  Pallas kernels: 81.3 us -> 78.5 us
    pallas_call x1, Pallas kernels: 81.3 us -> 78.5 us  [shards(): pl.pallas_call(functools.partial(kernel, nz, ny, td, scale), out_shape=(j...]
where the time goes in v4:
time: 80.9 us; the launch traced here: 80.8 us
  Pallas kernels  78.5 us (97%)
  other arithmetic  0.85 us (1%)
    pallas_call x1, Pallas kernels, shards(): pl.pallas_call(functools.partial(kernel, nz, ny, td, scale), out_shape=(j...  78.5 us

profile of v4, /device:TPU:1, one launch (start us, length us, event | category | flops | bytes accessed | tf_op | source)
XLA Modules:
  0.0 80.8 jit_solution(4797779807776199243)
XLA Ops:
  0.6 78.5 %shard_map.103 = (bf16[2,128,512]{2,1,0:T(8,128)(2,1)S(1)}, bf16[16,128,128]{2,1,0:T(8,128)(2,1)S(1)}) custom-call(bf16[2048,128]{1,0:T(8,128)(2,1)} %gp2.1, bf16[2048,128]{1,0:T(8,128)(2,1)} %agg2.1, bf16[128,512]{1,0:T(8,128)(2,1)} %w2.1, bf16[2048,128]{1,0:T(8,128)(2,1)} %pre1.1, bf16[2048,128]{1,0:T(8,128)(2,1)} %agg1.1, bf16[128,512]{1,0:T(8,128)(2,1)} %w1.1, ...), custom_call_target="tpu_custom_call" | custom-call | tf_op jit(solution)/shard_map/pallas_call | solution.py:449
  79.1 0.9 %bitcast_convert_fusion = (f32[128,512]{1,0:T(8,128)}, f32[128,512]{1,0:T(8,128)}) fusion(bf16[2,128,512]{2,1,0:T(8,128)(2,1)S(1)} %get-tuple-element.5), kind=kLoop, calls=%fused_computation | loop fusion | flops 131072 | bytes 786432 | tf_op jit(solution)/shard_map/convert_element_type | solution.py:508
  80.0 0.8 copy.12

commit v5 on v4

--- a/solution.py
+++ b/solution.py
@@ -22,7 +22,7 @@
     gw, gi,
     gath, blk, wv, pre, agg, aggt, prod, run, out, rec, giv, wacc, keys, slots, icols, fcols, tg, ints, floats,
     w1s, w1r, wzs, wzr, wys, wyr, wgs, wgr, wcr,
-    lsem, osem, gisem, gsend, grecv, ysend, yrecv, csend, crecv, zsend, zrecv, vsend, vrecv, tsend, trecv, c2send, c2recv,
+    lsem, osem, gisem, gsend, grecv, ysend, yrecv, csend, crecv, zsend, zrecv, vsend, vrecv, tsend, trecv, c2send, c2recv, usend, urecv,
 ):
     nb, tile, _ = blocks.shape
     bl = nb // td
@@ -74,7 +74,11 @@
     lax.fori_loop(1, nz, greet, 0)
 
     def greet_y(k, _):
-        pl.semaphore_signal(barrier, inc=1, device_id=ydev(lax.rem(y + k, ny)), device_id_type=MESH)
+        to = lax.rem(y + k, ny)
+        pl.semaphore_signal(barrier, inc=1, device_id=ydev(to), device_id_type=MESH)
+        pl.semaphore_signal(
+            barrier, inc=1, device_id=(z * (2 * ny) + to * 2 + 1 - core, x), device_id_type=MESH
+        )
         return 0
 
     lax.fori_loop(1, ny, greet_y, 0)
@@ -88,7 +92,7 @@
     w1_cp = fetch(w1, wv.at[1], 5)
     agg1_cp = fetch(agg1, agg.at[1], 6)
 
-    pl.semaphore_wait(barrier, 6 + nz - 1 + ny - 1)
+    pl.semaphore_wait(barrier, 6 + nz - 1 + 2 * (ny - 1))
 
     sends = []
 
@@ -329,6 +333,18 @@
             total = total + wyr[l, k].astype(F32)
         wgs[l] = total.astype(BF)
         others(side, at_a[l], gout(l))
+        if l == 1:
+            across(y).start()
+            others(side, y, across)
+
+    def yboth(k):
+        return (z * (2 * ny) + k * 2 + 1 - core, x)
+
+    def across(k):
+        return remote(wgs.at[1], wcr.at[1, piece(y)], usend.at[k], urecv.at[y], yboth(k))
+
+    def across_in(k):
+        return remote(wgs.at[1], wcr.at[1, piece(k)], usend.at[k], urecv.at[k], yboth(k))
 
     def c2copy(l):
         return wgr.at[l], wcr.at[l], c2send.at[l], c2recv.at[l], partner
@@ -344,11 +360,16 @@
     def weight5(l):
         wgr[l, piece(at_a[l])] = wgs[l]
         all_recv(side, at_a[l], gin(l))
-        send(*c2copy(l))
+        if l == 0:
+            send(*c2copy(l))
         put_weight(l, core, wgr, 0)
 
     def weight6(l):
-        remote(*c2copy(l)).wait_recv()
+        if l == 0:
+            remote(*c2copy(l)).wait_recv()
+        else:
+            across_in(y).wait_recv()
+            all_recv(side, y, across_in)
         put_weight(l, 1 - core, wcr, 1)
 
     evens, odds = list(range(0, chunks, 2)), list(range(1, chunks, 2))
@@ -421,6 +442,8 @@
     weight5(1)
     weight6(1)
     all_sent(side, at_a[1], gin(1))
+    across_in(y).wait_send()
+    all_sent(side, y, across_in)
     for cp in sends:
         cp.wait_send()
     for cp in outs:
@@ -500,6 +523,8 @@
             dma((2, nz)),
             dma((2,)),
             dma((2,)),
+            dma((ny,)),
+            dma((ny,)),
         ],
         compiler_params=pltpu.CompilerParams(
             collective_id=0, has_side_effects=True, vmem_limit_bytes=40 * 1024 * 1024

time: 80.9 us -> 80.5 us (level)
  no operation moved by 1% of the time
where the time goes in v5:
time: 80.5 us; the launch traced here: 80.4 us
  Pallas kernels  78.1 us (97%)
  other arithmetic  0.85 us (1%)
    pallas_call x1, Pallas kernels, shards(): pl.pallas_call(functools.partial(kernel, nz, ny, td, scale), out_shape=(j...  78.1 us

profile of v5, /device:TPU:1, one launch (start us, length us, event | category | flops | bytes accessed | tf_op | source)
XLA Modules:
  0.0 80.4 jit_solution(17849026329549035922)
XLA Ops:
  0.6 78.1 %shard_map.103 = (bf16[2,128,512]{2,1,0:T(8,128)(2,1)S(1)}, bf16[16,128,128]{2,1,0:T(8,128)(2,1)S(1)}) custom-call(bf16[2048,128]{1,0:T(8,128)(2,1)} %gp2.1, bf16[2048,128]{1,0:T(8,128)(2,1)} %agg2.1, bf16[128,512]{1,0:T(8,128)(2,1)} %w2.1, bf16[2048,128]{1,0:T(8,128)(2,1)} %pre1.1, bf16[2048,128]{1,0:T(8,128)(2,1)} %agg1.1, bf16[128,512]{1,0:T(8,128)(2,1)} %w1.1, ...), custom_call_target="tpu_custom_call" | custom-call | tf_op jit(solution)/shard_map/pallas_call | solution.py:472
  78.8 0.9 %bitcast_convert_fusion = (f32[128,512]{1,0:T(8,128)}, f32[128,512]{1,0:T(8,128)}) fusion(bf16[2,128,512]{2,1,0:T(8,128)(2,1)S(1)} %get-tuple-element.5), kind=kLoop, calls=%fused_computation | loop fusion | flops 131072 | bytes 786432 | tf_op jit(solution)/shard_map/convert_element_type | solution.py:533
  79.6 0.8 copy.12
